TPU v7x, 32 devices: a whole 2x2x4 slice. The times are simulated.
32 devices in a mesh: dp: 8 (over z, y), mp: 4 (over x, core).
Axes of the slice: x: 2, y: 2, z: 4, core: 2. Of those that a mesh axis runs over, the one named last changes fastest.
Arguments:
- frames: bfloat16 [2048, 1024], P('dp'), may hold values from -24 to 24
- proj_in: bfloat16 [1024, 2, 1024], P(None, None, 'mp'), may hold values from -0.1875 to 0.1875
- depthwise: float32 [31, 1024], P(None, 'mp'), may hold values from -1 to 1
- bn_gain: float32 [1024], P('mp'), may hold values from 0.5 to 1.5
- bn_shift: float32 [1024], P('mp'), may hold values from -3 to 3
- proj_out: bfloat16 [1024, 1024], P(None, 'mp'), may hold values from -0.1875 to 0.1875
- grad_out: bfloat16 [2048, 1024], P('dp'), may hold values from -6 to 6
- counts: int32 [8], replicated, may hold values from 1 to 2, as said below
- lengths: int32 [8, 2], P('dp'), may hold values from 1 to 255, as said below
Outputs:
- frame_grad: bfloat16 [2048, 1024], P('dp', 'mp')
- in_grad: float32 [1024, 2, 1024], P('dp', None, 'mp')
- out_grad: float32 [1024, 1024], P('dp', 'mp')
- depth_grad: float32 [31, 1024], P(None, 'mp')
- gain_grad: float32 [1024], P('mp')
- shift_grad: float32 [1024], P('mp')
Inputs may be any that keep to these rules, and one draw needn't show every extreme that they name: `counts`: some device holds 2 live blocks. lengths[d] sums to 128 * counts[d]; on some device with 2 live blocks one utterance holds all frames but one for each other utterance.
All inputs are finite; a program needn't handle non-finite values.
Results may differ from a plain program's by a relative error of at most 0.0095.
Values may be sent and summed in bfloat16 or wider, within the bound.
A program may use at most 64 MiB of HBM per device.

v0:
```python
import jax
import jax.numpy as jnp
from jax import lax
from jax.sharding import PartitionSpec as P

BLOCK = 128


def time_shift(values, offset, fill_value):
    if offset > 0:
        pad_part = jnp.full((offset,) + values.shape[1:], fill_value, values.dtype)
        return jnp.concatenate([values[offset:], pad_part], axis=0)
    if offset < 0:
        pad_part = jnp.full((-offset,) + values.shape[1:], fill_value, values.dtype)
        return jnp.concatenate([pad_part, values[:offset]], axis=0)
    return values


def tap_term(glu_float, owner_id, live_col, offset):
    same_utt = (time_shift(owner_id, offset, -1) == owner_id).astype(jnp.float32)[
        :, None
    ] * live_col
    return time_shift(glu_float, offset, 0.0) * same_utt


def shards(frames, proj_in, depthwise, bn_gain, bn_shift, proj_out, grad_out, counts, lengths):
    frames_dev = frames.shape[0]
    model_width = frames.shape[1]
    channels = proj_in.shape[2]
    tap_count = depthwise.shape[0]
    radius = tap_count // 2
    rows_dev = model_width // lax.axis_size("dp")
    position = jnp.arange(frames_dev, dtype=jnp.int32)
    utt_ends = jnp.cumsum(lengths[0])
    owner_id = jnp.sum((position[:, None] >= utt_ends[None, :]).astype(jnp.int32), axis=1)
    my_count = counts[lax.axis_index("dp")]
    live_col = (position < my_count * BLOCK).astype(jnp.float32)[:, None]
    frame_total = (jnp.sum(counts) * BLOCK).astype(jnp.float32)
    proj_flat = proj_in.reshape(model_width, 2 * channels)
    pre_act = jnp.dot(frames, proj_flat, preferred_element_type=jnp.float32)
    value_half = pre_act[:, :channels]
    gate_sig = jax.nn.sigmoid(pre_act[:, channels:])
    glu_out = (value_half * gate_sig * live_col).astype(jnp.bfloat16)
    glu_float = lax.optimization_barrier(glu_out).astype(jnp.float32)
    conv_out = jnp.zeros((frames_dev, channels), jnp.float32)
    for tap_index in range(tap_count):
        conv_out = conv_out + depthwise[tap_index] * tap_term(
            glu_float, owner_id, live_col, tap_index - radius
        )
    sum_val, sum_sq = lax.psum(
        (jnp.sum(conv_out, axis=0), jnp.sum(conv_out * conv_out, axis=0)), "dp"
    )
    mean_val = sum_val / frame_total
    square_mean = sum_sq / frame_total
    inv_std = lax.rsqrt(square_mean - mean_val * mean_val + 1e-05)
    normed = (conv_out - mean_val) * inv_std
    scaled = normed * bn_gain + bn_shift
    sig_scaled = jax.nn.sigmoid(scaled)
    hidden = (scaled * sig_scaled * live_col).astype(jnp.bfloat16)
    grad_hidden = jnp.dot(grad_out, proj_out, preferred_element_type=jnp.float32) * live_col
    grad_scaled = grad_hidden * sig_scaled * (1.0 + scaled * (1.0 - sig_scaled))
    local_shift = jnp.sum(grad_scaled, axis=0)
    local_gain = jnp.sum(grad_scaled * normed, axis=0)
    shift_grad, gain_grad = lax.psum((local_shift, local_gain), "dp")
    grad_conv = (
        live_col
        * bn_gain
        * inv_std
        * (grad_scaled - shift_grad / frame_total - normed * gain_grad / frame_total)
    )
    depth_rows = []
    for tap_index in range(tap_count):
        depth_rows.append(
            jnp.sum(grad_conv * tap_term(glu_float, owner_id, live_col, tap_index - radius), axis=0)
        )
    depth_grad = lax.psum(jnp.stack(depth_rows), "dp")
    grad_glu = jnp.zeros((frames_dev, channels), jnp.float32)
    for tap_index in range(tap_count):
        offset = tap_index - radius
        back_same = (time_shift(owner_id, -offset, -1) == owner_id).astype(jnp.float32)[
            :, None
        ] * live_col
        grad_glu = grad_glu + depthwise[tap_index] * time_shift(grad_conv, -offset, 0.0) * back_same
    grad_value = grad_glu * gate_sig
    grad_gate = grad_glu * value_half * gate_sig * (1.0 - gate_sig)
    grad_flat = jnp.concatenate([grad_value, grad_gate], axis=1).astype(jnp.bfloat16)
    frame_term = lax.dot_general(
        grad_flat, proj_flat, (((1,), (1,)), ((), ())), preferred_element_type=jnp.float32
    )
    frame_grad = lax.psum_scatter(
        frame_term.astype(jnp.bfloat16), "mp", scatter_dimension=1, tiled=True
    )
    summed = lax.psum_scatter(
        jnp.concatenate(
            [
                lax.dot_general(
                    frames, grad_flat, (((0,), (0,)), ((), ())), preferred_element_type=jnp.float32
                ),
                lax.dot_general(
                    grad_out, hidden, (((0,), (0,)), ((), ())), preferred_element_type=jnp.float32
                ),
            ],
            axis=1,
        ),
        "dp",
        scatter_dimension=0,
        tiled=True,
    )
    in_flat = summed[:, : 2 * channels]
    out_grad = summed[:, 2 * channels :]
    in_grad = in_flat.reshape(rows_dev, 2, channels)
    return (frame_grad, in_grad, out_grad, depth_grad, gain_grad, shift_grad)


def solution(mesh):
    placed = (
        P("dp", None),
        P(None, None, "mp"),
        P(None, "mp"),
        P("mp"),
        P("mp"),
        P(None, "mp"),
        P("dp", None),
        P(),
        P("dp", None),
    )
    return jax.shard_map(
        shards,
        mesh=mesh,
        in_specs=placed,
        out_specs=(
            P("dp", "mp"),
            P("dp", None, "mp"),
            P("dp", "mp"),
            P(None, "mp"),
            P("mp"),
            P("mp"),
        ),
        check_vma=False,
    )
```

profile of v0, /device:TPU:0, one launch (start us, length us, event | category | flops | bytes accessed | tf_op | source)
XLA Modules:
  0.0 209.4 jit_solution(8868557519326809147)
XLA Ops:
  7.2 0.9 reduce-window.8
  8.2 0.6 fusion.86
  9.4 0.7 fusion.85
  10.7 0.7 fusion.84
  11.4 0.7 fusion.90
  12.0 0.7 fusion.83
  17.8 1.6 fusion.78
  19.4 1.7 fusion.77
  21.1 1.3 reduce_sum.335
  22.4 1.2 dynamic_slice.3
  24.3 1.5 copy.19
  26.3 0.8 fusion.69
  27.1 0.9 fusion.68
  28.0 0.8 fusion.67
  28.8 0.8 fusion.66
  29.6 0.8 fusion.65
  30.4 0.8 fusion.64
  31.3 0.8 fusion.63
  32.1 0.8 fusion.62
  32.9 0.7 fusion.71
  33.7 0.7 fusion.70
  34.4 0.7 fusion.73
  35.2 0.7 fusion.72
  35.9 0.8 fusion.76
  36.7 0.8 fusion.75
  37.6 0.8 fusion.74
  38.9 0.9 fusion.14
  39.9 0.9 fusion.13
  41.0 6.2 %multiply_reduce_fusion.32 = (f32[256]{0:T(256)S(1)}, f32[256]{0:T(256)}, f32[256,256]{1,0:T(8,128)}) fusion(f32[256]{0:T(256)S(1)} %get-tuple-element.155, f32[241,256]{1,0:T(8,128)} %get-tuple-element.94, f32[256]{0:T(256)} %bitcast.103, f32[256]{0:T(256)S(1)} %get-tuple-element.156, f32[242,256]{1,0:T(8,128)} %get-tuple-element.96, f32[256]{0:T(256)} %bitcast.105, ...), kind=kLoop, calls=%fused_computation.52 | loop fusion | flops 6290944 | bytes 8077312 | tf_op jit(solution)/shard_map/reduce_sum | solution.py:51
  47.5 23.3 %all-reduce.89 = (f32[256]{0:T(256)S(1)}, f32[256]{0:T(256)S(1)}) all-reduce(f32[256]{0:T(256)} %get-tuple-element.52, f32[256]{0:T(256)S(1)} %get-tuple-element.51), channel_id=1, replica_groups=mesh['dp'=8,'mp'=4] {'dp'}, use_global_device_ids=true, to_apply=%region_6.7 | all-reduce | flops 512 | bytes 4096 | tf_op jit(solution)/shard_map/psum | solution.py:50
  70.8 2.3 %fusion.46 = (f32[256]{0:T(256)S(1)}, f32[256]{0:T(256)S(1)}, f32[256,256]{1,0:T(8,128)}) fusion(f32[256]{0:T(256)S(1)} %get-tuple-element.60, f32[256,256]{1,0:T(8,128)} %get-tuple-element.62, f32[256]{0:T(256)S(1)} %get-tuple-element.61, f32[256]{0:T(256)} %param.13, f32[256]{0:T(256)} %param.12, f32[256]{0:T(256)S(1)} %fusion.42, ...), kind=kOutput, calls=%fused_computation.162 | convolution fusion | flops 135265792 | bytes 1580032 | tf_op jit(solution)/shard_map/dot_general | solution.py:60
  73.1 17.7 %all-reduce.88 = (f32[256]{0:T(256)}, f32[256]{0:T(256)S(1)}) all-reduce(f32[256]{0:T(256)S(1)} %get-tuple-element.50, f32[256]{0:T(256)S(1)} %get-tuple-element.49), channel_id=1, replica_groups=mesh['dp'=8,'mp'=4] {'dp'}, use_global_device_ids=true, to_apply=%region_10.11 | all-reduce | flops 512 | bytes 4096 | tf_op jit(solution)/shard_map/psum | solution.py:64
  91.3 2.9 %multiply_reduce_fusion = (f32[256]{0:T(256)}, f32[256]{0:T(256)}, f32[256]{0:T(256)}, f32[256]{0:T(256)}, f32[256]{0:T(256)}, /*index=5*/f32[256]{0:T(256)}, f3...) fusion(f32[241,256]{1,0:T(8,128)} %get-tuple-element.94, f32[256]{0:T(256)S(1)} %get-tuple-element.155, ...), kind=kLoop, calls=%fused_computation.12 | loop fusion | flops 2356992 | bytes 3068932 | tf_op jit(solution)/shard_map/reduce_sum | solution.py:74
  95.6 1.5 convolution_bitcast_fusion.1
  97.5 3.4 %multiply_convert_fusion.2 = (bf16[256,256]{1,0:T(8,128)(2,1)S(1)}, f32[256,256]{1,0:T(8,128)S(1)}) fusion(f32[256,512]{1,0:T(8,128)S(1)} %fusion.94, f32[256]{0:T(256)S(1)} %copy-done.58, f32[241,256]{1,0:T(8,128)S(1)} %get-tuple-element.64, f32[256]{0:T(256)S(1)} %bitcast.104, f32[256]{0:T(256)S(1)} %copy-done.72, f32[242,256]{1,0:T(8,128)S(1)} %get-tuple-element.66, ...), kind=kLoop, calls=%fused_computation.45 | loop fusion | flops 6356992 | bytes 8599552 | tf_op jit(solution)/shard_map/convert
  102.1 1.9 pad_maximum_fusion
  104.0 2.3 %convolution_convert_fusion = bf16[256,1024]{1,0:T(8,128)(2,1)} fusion(bf16[1024,512]{1,0:T(8,128)(2,1)S(1)} %bitcast.80, bf16[256,256]{1,0:T(8,128)(2,1)} %copy-done.11, bf16[256,256]{1,0:T(8,128)(2,1)} %copy-done.12), kind=kOutput, calls=%fused_computation.3 | convolution fusion | flops 269221888 | bytes 1835008 | tf_op jit(solution)/shard_map/dot_general | solution.py:87
  106.4 2.3 %multiply_reduce_fusion.27 = (f32[256]{0:T(256)}, f32[256]{0:T(256)}, f32[256]{0:T(256)}, f32[256]{0:T(256)}) fusion(f32[256,256]{1,0:T(8,128)S(1)} %get-tuple-element.57, f32[244,256]{1,0:T(8,128)} %get-tuple-element.99, f32[256]{0:T(256)} %copy-done.55, f32[256]{0:T(256)} %copy-done.53, f32[243,256]{1,0:T(8,128)} %get-tuple-element.97, f32[256]{0:T(256)} %copy-done.71, ...), kind=kLoop, calls=%fused_computation.39 | loop fusion | flops 785408 | bytes 1263616 | tf_op jit(solution)/shard_map/reduce_sum | solution.py:74
  108.7 2.6 %multiply_reduce_fusion.18 = (f32[256]{0:T(256)}, f32[256]{0:T(256)}, f32[256]{0:T(256)}, f32[256]{0:T(256)}, f32[256]{0:T(256)}, /*index=5*/f32[256]{0:T(256)}, f32[256]{0:T(256)}, f32[256]{0:T(256)}, f32[256]{0:T(256)}) fusion(f32[256,256]{1,0:T(8,128)S(1)} %get-tuple-element.57, f32[253,256]{1,0:T(8,128)S(1)} %copy-done.2, f32[256]{0:T(256)S(1)} %copy-done.36, ...), kind=kLoop, calls=%fused_computation.30 | loop fusion | flops 1767168 | bytes 2575360 | tf_op jit(solution)/shard_map/reduce_sum | solution.py:74
  111.4 1.1 multiply_reduce_fusion.9
  112.5 2.9 %stack.127 = f32[31,256]{1,0:T(8,128)S(1)} concatenate(f32[1,256]{1,0:T(1,128)} %bitcast.157, f32[1,256]{1,0:T(1,128)} %bitcast.156, f32[1,256]{1,0:T(1,128)} %bitcast.155, f32[1,256]{1,0:T(1,128)} %bitcast.154, f32[1,256]{1,0:T(1,128)} %bitcast.166, f32[1,256]{1,0:T(1,128)} %bitcast.165, f32[1,256]{1,0:T(1,128)} %bitcast.164, f32[1,256]{1,0:T(1,128)} %bitcast.163, ...), dimensions={0} | concatenate | bytes 63488 | tf_op jit(solution)/shard_map/stack | solution.py:76
  115.4 36.4 %psum.39 = f32[31,256]{1,0:T(8,128)} all-reduce(f32[31,256]{1,0:T(8,128)S(1)} %stack.127), channel_id=1, replica_groups=mesh['dp'=8,'mp'=4] {'dp'}, use_global_device_ids=true, to_apply=%region_44.45 | all-reduce | flops 7936 | bytes 63488 | tf_op jit(solution)/shard_map/psum | solution.py:76
  151.8 26.7 %reduce-scatter.5.cloned.1.call-done = f32[128,768]{0,1:T(8,128)} async-done(((f32[1024,768]{0,1:T(8,128)}), f32[128,768]{0,1:T(8,128)}) %reduce-scatter.5.cloned.1.call-update) | async-done | bytes 393232 | tf_op jit(solution)/shard_map/reduce_scatter | solution.py:93
  178.5 1.0 slice.683
  179.4 0.8 copy.17
  180.3 0.9 slice.684
  181.2 0.8 copy.18
  182.0 20.6 %reduce-scatter.3.cloned.1.call-done = bf16[256,256]{1,0:T(8,128)(2,1)} async-done(((bf16[256,1024]{1,0:T(8,128)(2,1)}), bf16[256,256]{1,0:T(8,128)(2,1)}) %reduce-scatter.3.cloned.1.call-update) | async-done | bytes 131088 | tf_op jit(solution)/shard_map/reduce_scatter | solution.py:90
  (211 shorter events, 10.0 us)
Async XLA Ops:
  7.2 18.6 %copy-start = (bf16[256,1024]{1,0:T(8,128)(2,1)S(1)}, bf16[256,1024]{1,0:T(8,128)(2,1)}, u32[]{:S(2)}) copy-start(bf16[256,1024]{1,0:T(8,128)(2,1)} %param.9) | copy-start | bytes 1572868
  7.2 171.3 %reduce-scatter.5.cloned.1.call-start = ((), (), s32[]{:S(2)}) async-start(), calls=%async_computation.3 | async-start | bytes 3538944 | tf_op jit(solution)/shard_map/reduce_scatter | solution.py:93
  38.3 8.9 %copy-start.1 = (f32[253,256]{1,0:T(8,128)}, f32[253,256]{1,0:T(8,128)S(1)}, u32[]{:S(2)}) copy-start(f32[253,256]{1,0:T(8,128)S(1)} %get-tuple-element.117) | copy-start | bytes 777220
  39.8 7.4 %copy-start.28 = (f32[256]{0:T(256)}, f32[256]{0:T(256)S(1)}, u32[]{:S(2)}) copy-start(f32[256]{0:T(256)S(1)} %get-tuple-element.173) | copy-start | bytes 3076
  39.8 7.4 %copy-start.31 = (f32[256]{0:T(256)}, f32[256]{0:T(256)S(1)}, u32[]{:S(2)}) copy-start(f32[256]{0:T(256)S(1)} %get-tuple-element.174) | copy-start | bytes 3076
  39.8 7.4 %copy-start.34 = (f32[256]{0:T(256)}, f32[256]{0:T(256)S(1)}, u32[]{:S(2)}) copy-start(f32[256]{0:T(256)S(1)} %get-tuple-element.175) | copy-start | bytes 3076
  39.8 7.4 %copy-start.37 = (f32[256]{0:T(256)}, f32[256]{0:T(256)S(1)}, u32[]{:S(2)}) copy-start(f32[256]{0:T(256)S(1)} %get-tuple-element.176) | copy-start | bytes 3076
  39.8 7.4 %copy-start.39 = (f32[256]{0:T(256)}, f32[256]{0:T(256)S(1)}, u32[]{:S(2)}) copy-start(f32[256]{0:T(256)S(1)} %get-tuple-element.177) | copy-start | bytes 3076
  39.9 7.4 %copy-start.41 = (f32[256]{0:T(256)}, f32[256]{0:T(256)S(1)}, u32[]{:S(2)}) copy-start(f32[256]{0:T(256)S(1)} %get-tuple-element.178) | copy-start | bytes 3076
  39.9 7.4 %copy-start.43 = (f32[256]{0:T(256)}, f32[256]{0:T(256)S(1)}, u32[]{:S(2)}) copy-start(f32[256]{0:T(256)S(1)} %get-tuple-element.179) | copy-start | bytes 3076
  39.9 7.4 %copy-start.45 = (f32[256]{0:T(256)}, f32[256]{0:T(256)S(1)}, u32[]{:S(2)}) copy-start(f32[256]{0:T(256)S(1)} %get-tuple-element.180) | copy-start | bytes 3076
  39.9 7.4 %copy-start.47 = (f32[256]{0:T(256)}, f32[256]{0:T(256)S(1)}, u32[]{:S(2)}) copy-start(f32[256]{0:T(256)S(1)} %get-tuple-element.181) | copy-start | bytes 3076
  39.9 7.4 %copy-start.49 = (f32[256]{0:T(256)}, f32[256]{0:T(256)S(1)}, u32[]{:S(2)}) copy-start(f32[256]{0:T(256)S(1)} %get-tuple-element.182) | copy-start | bytes 3076
  39.9 7.4 %copy-start.51 = (f32[256]{0:T(256)}, f32[256]{0:T(256)S(1)}, u32[]{:S(2)}) copy-start(f32[256]{0:T(256)S(1)} %get-tuple-element.183) | copy-start | bytes 3076
  39.9 7.4 %copy-start.53 = (f32[256]{0:T(256)}, f32[256]{0:T(256)S(1)}, u32[]{:S(2)}) copy-start(f32[256]{0:T(256)S(1)} %get-tuple-element.172) | copy-start | bytes 3076
  39.9 7.4 %copy-start.55 = (f32[256]{0:T(256)}, f32[256]{0:T(256)S(1)}, u32[]{:S(2)}) copy-start(f32[256]{0:T(256)S(1)} %get-tuple-element.184) | copy-start | bytes 3076
  39.9 7.4 %copy-start.57 = (f32[256]{0:T(256)}, f32[256]{0:T(256)S(1)}, u32[]{:S(2)}) copy-start(f32[256]{0:T(256)S(1)} %get-tuple-element.185) | copy-start | bytes 3076
  40.8 6.5 %copy-start.14 = (f32[256]{0:T(256)}, f32[256]{0:T(256)S(1)}, u32[]{:S(2)}) copy-start(f32[256]{0:T(256)S(1)} %get-tuple-element.157) | copy-start | bytes 3076
  40.8 6.5 %copy-start.16 = (f32[256]{0:T(256)}, f32[256]{0:T(256)S(1)}, u32[]{:S(2)}) copy-start(f32[256]{0:T(256)S(1)} %get-tuple-element.158) | copy-start | bytes 3076
  40.9 6.5 %copy-start.18 = (f32[256]{0:T(256)}, f32[256]{0:T(256)S(1)}, u32[]{:S(2)}) copy-start(f32[256]{0:T(256)S(1)} %get-tuple-element.159) | copy-start | bytes 3076
  40.9 6.5 %copy-start.20 = (f32[256]{0:T(256)}, f32[256]{0:T(256)S(1)}, u32[]{:S(2)}) copy-start(f32[256]{0:T(256)S(1)} %get-tuple-element.160) | copy-start | bytes 3076
  40.9 6.5 %copy-start.22 = (f32[256]{0:T(256)}, f32[256]{0:T(256)S(1)}, u32[]{:S(2)}) copy-start(f32[256]{0:T(256)S(1)} %get-tuple-element.161) | copy-start | bytes 3076
  40.9 6.5 %copy-start.24 = (f32[256]{0:T(256)}, f32[256]{0:T(256)S(1)}, u32[]{:S(2)}) copy-start(f32[256]{0:T(256)S(1)} %get-tuple-element.162) | copy-start | bytes 3076
  40.9 6.5 %copy-start.26 = (f32[256]{0:T(256)}, f32[256]{0:T(256)S(1)}, u32[]{:S(2)}) copy-start(f32[256]{0:T(256)S(1)} %get-tuple-element.163) | copy-start | bytes 3076
  40.9 6.5 %copy-start.59 = (f32[256]{0:T(256)}, f32[256]{0:T(256)S(1)}, u32[]{:S(2)}) copy-start(f32[256]{0:T(256)S(1)} %get-tuple-element.164) | copy-start | bytes 3076
  40.9 6.5 %copy-start.61 = (f32[256]{0:T(256)}, f32[256]{0:T(256)S(1)}, u32[]{:S(2)}) copy-start(f32[256]{0:T(256)S(1)} %get-tuple-element.165) | copy-start | bytes 3076
  40.9 6.5 %copy-start.63 = (f32[256]{0:T(256)}, f32[256]{0:T(256)S(1)}, u32[]{:S(2)}) copy-start(f32[256]{0:T(256)S(1)} %get-tuple-element.166) | copy-start | bytes 3076
  40.9 6.5 %copy-start.65 = (f32[256]{0:T(256)}, f32[256]{0:T(256)S(1)}, u32[]{:S(2)}) copy-start(f32[256]{0:T(256)S(1)} %get-tuple-element.167) | copy-start | bytes 3076
  40.9 6.5 %copy-start.67 = (f32[256]{0:T(256)}, f32[256]{0:T(256)S(1)}, u32[]{:S(2)}) copy-start(f32[256]{0:T(256)S(1)} %get-tuple-element.168) | copy-start | bytes 3076
  41.0 6.5 %copy-start.69 = (f32[256]{0:T(256)}, f32[256]{0:T(256)S(1)}, u32[]{:S(2)}) copy-start(f32[256]{0:T(256)S(1)} %get-tuple-element.169) | copy-start | bytes 3076
  41.0 6.5 %copy-start.71 = (f32[256]{0:T(256)}, f32[256]{0:T(256)S(1)}, u32[]{:S(2)}) copy-start(f32[256]{0:T(256)S(1)} %get-tuple-element.154) | copy-start | bytes 3076
  70.7 20.0 %copy-start.84 = (f32[256]{0:T(256)}, f32[256]{0:T(256)S(1)}, u32[]{:S(2)}) copy-start(f32[256]{0:T(256)S(1)} %get-tuple-element.60) | copy-start | bytes 3076
  70.7 20.0 %copy-start.85 = (f32[256]{0:T(256)}, f32[256]{0:T(256)S(1)}, u32[]{:S(2)}) copy-start(f32[256]{0:T(256)S(1)} %get-tuple-element.61) | copy-start | bytes 3076
  94.7 2.3 %copy-start.15 = (f32[256]{0:T(256)S(1)}, f32[256]{0:T(256)}, u32[]{:S(2)}) copy-start(f32[256]{0:T(256)} %copy-done.14) | copy-start | bytes 3076
  94.7 2.3 %copy-start.17 = (f32[256]{0:T(256)S(1)}, f32[256]{0:T(256)}, u32[]{:S(2)}) copy-start(f32[256]{0:T(256)} %copy-done.16) | copy-start | bytes 3076
  103.9 4.8 %copy-start.2 = (f32[253,256]{1,0:T(8,128)S(1)}, f32[253,256]{1,0:T(8,128)}, u32[]{:S(2)}) copy-start(f32[253,256]{1,0:T(8,128)} %copy-done.1) | copy-start | bytes 777220
  103.9 4.8 %copy-start.36 = (f32[256]{0:T(256)S(1)}, f32[256]{0:T(256)}, u32[]{:S(2)}) copy-start(f32[256]{0:T(256)} %copy-done.34) | copy-start | bytes 3076
  104.0 7.4 %copy-start.3 = (f32[250,256]{1,0:T(8,128)S(1)}, f32[250,256]{1,0:T(8,128)}, u32[]{:S(2)}) copy-start(f32[250,256]{1,0:T(8,128)} %get-tuple-element.112) | copy-start | bytes 768004
  104.0 7.4 %copy-start.30 = (f32[256]{0:T(256)S(1)}, f32[256]{0:T(256)}, u32[]{:S(2)}) copy-start(f32[256]{0:T(256)} %copy-done.28) | copy-start | bytes 3076
  104.0 7.4 %copy-start.33 = (f32[256]{0:T(256)S(1)}, f32[256]{0:T(256)}, u32[]{:S(2)}) copy-start(f32[256]{0:T(256)} %copy-done.31) | copy-start | bytes 3076
  104.0 98.6 %reduce-scatter.3.cloned.1.call-start = ((), (), s32[]{:S(2)}) async-start(), calls=%async_computation.2 | async-start | bytes 655360 | tf_op jit(solution)/shard_map/reduce_scatter | solution.py:90
  106.3 5.0 %copy-start.4 = (f32[252,256]{1,0:T(8,128)S(1)}, f32[252,256]{1,0:T(8,128)}, u32[]{:S(2)}) copy-start(f32[252,256]{1,0:T(8,128)} %get-tuple-element.116) | copy-start | bytes 774148
  106.3 5.1 %copy-start.5 = (f32[251,256]{1,0:T(8,128)S(1)}, f32[251,256]{1,0:T(8,128)}, u32[]{:S(2)}) copy-start(f32[251,256]{1,0:T(8,128)} %get-tuple-element.114) | copy-start | bytes 771076
  106.3 5.1 %copy-start.6 = (f32[255,256]{1,0:T(8,128)S(1)}, f32[255,256]{1,0:T(8,128)}, u32[]{:S(2)}) copy-start(f32[255,256]{1,0:T(8,128)} %get-tuple-element.121) | copy-start | bytes 783364
  106.3 5.1 %copy-start.7 = (f32[255,256]{1,0:T(8,128)S(1)}, f32[255,256]{1,0:T(8,128)}, u32[]{:S(2)}) copy-start(f32[255,256]{1,0:T(8,128)} %get-tuple-element.122) | copy-start | bytes 783364
  106.4 5.0 %copy-start.8 = (f32[254,256]{1,0:T(8,128)S(1)}, f32[254,256]{1,0:T(8,128)}, u32[]{:S(2)}) copy-start(f32[254,256]{1,0:T(8,128)} %get-tuple-element.119) | copy-start | bytes 780292
  106.4 5.0 %copy-start.9 = (f32[254,256]{1,0:T(8,128)S(1)}, f32[254,256]{1,0:T(8,128)}, u32[]{:S(2)}) copy-start(f32[254,256]{1,0:T(8,128)} %get-tuple-element.120) | copy-start | bytes 780292
  106.4 5.0 %copy-start.10 = (f32[253,256]{1,0:T(8,128)S(1)}, f32[253,256]{1,0:T(8,128)}, u32[]{:S(2)}) copy-start(f32[253,256]{1,0:T(8,128)} %get-tuple-element.118) | copy-start | bytes 777220
  (41 other events, 89.4 us)
Sparse Core Ops, SparseCore 0:
  104.1 74.3 reduce-scatter.4
  181.5 20.9 reduce-scatter.2
where the time goes:
time: 210 us; the launch traced here: 209 us
  blocking collectives  77.3 us (37%)
  waiting for transfers between devices  47.4 us (23%)
  local copies, waits for them, and re-layouts  36.3 us (17%)
  other arithmetic  24.7 us (12%)
  between operations  16.7 us (8%)
  matrix products  6.97 us (3%)
    psum x1, blocking collectives, shards(): depth_grad = lax.psum(jnp.stack(depth_rows), 'dp')  36.4 us
    reduce_scatter x1, waiting for transfers between devices, shards(): lax.psum_scatter(jnp.concatenate([lax.dot_general(frames, grad_flat, (((0...  26.7 us
    psum x1, blocking collectives, shards(): lax.psum((jnp.sum(conv_out, axis=0), jnp.sum(conv_out * conv_out, axis=0)...  23.3 us
    slice x29, local copies, waits for them, and re-layouts, time_shift(): return jnp.concatenate([pad_part, values[:offset]], axis=0)  21 us
    reduce_scatter x1, waiting for transfers between devices, shards(): lax.psum_scatter(frame_term.astype(jnp.bfloat16), 'mp', scatter_dimension...  20.6 us
    psum x1, blocking collectives, shards(): shift_grad, gain_grad = lax.psum((local_shift, local_gain), 'dp')  17.7 us
    reduce_sum x4, other arithmetic, shards(): jnp.sum(grad_conv * tap_term(glu_float, owner_id, live_col, tap_index - r...  9.01 us
    reduce_sum x1, other arithmetic, shards(): jnp.sum(conv_out * conv_out, axis=0)  6.23 us
  transfers between devices with their start and end apart: 2, of which 2 were waited for; matrix products, arithmetic and copies ran while one was open for 7% of the time, Pallas kernels for 0%

commit v1 on v0

--- a/solution.py
+++ b/solution.py
@@ -1,6 +1,10 @@
+import functools
+
 import jax
 import jax.numpy as jnp
 from jax import lax
+from jax.experimental import pallas as pl
+from jax.experimental.pallas import tpu as pltpu
 from jax.sharding import PartitionSpec as P
 
 BLOCK = 128
@@ -112,6 +116,342 @@
     return (frame_grad, in_grad, out_grad, depth_grad, gain_grad, shift_grad)
 
 
+GAP = 16
+NT = (((1,), (1,)), ((), ()))
+TN = (((0,), (0,)), ((), ()))
+
+
+def dot(a, b, dims=(((1,), (0,)), ((), ()))):
+    return lax.dot_general(a, b, dims, preferred_element_type=jnp.float32)
+
+
+def remote(src, dst, send_sem, recv_sem, dp, mp):
+    return pltpu.make_async_remote_copy(
+        src_ref=src,
+        dst_ref=dst,
+        send_sem=send_sem,
+        recv_sem=recv_sem,
+        device_id=(dp, mp),
+        device_id_type=pl.DeviceIdType.MESH,
+    )
+
+
+def fused(
+    n_dp, n_mp,
+    frames, proj, taps, gain, shift, proj_out, grad_out, counts, lengths,
+    o_frame, o_in, o_out, o_depth, o_gain, o_shift,
+    place, live, fg, gg, gpad, cpad, val, gate, conv, gh, gs, gp,
+    st1, st1_s, st1_r, st2, st2_s, st2_r,
+    oy_s, oy_r, okeep, oz_s, oz_r, oys_sem, oyr_sem, ozs_sem, ozr_sem,
+    iy_s, iy_r, ikeep, iz_s, iz_r, iys_sem, iyr_sem, izs_sem, izr_sem,
+    f_s, f_r, fs_sem, fr_sem,
+    d_s, d_r, ds_sem, dr_sem, e_r, es_sem, er_sem,
+):
+    rows, chans = conv.shape
+    slots = frames.shape[0]
+    tap_count = taps.shape[0]
+    radius = tap_count // 2
+    me = lax.axis_index("dp")
+    mp = lax.axis_index("mp")
+    nz = n_dp // 2
+    my_y = lax.rem(me, 2)
+    my_z = me // 2
+    piece = o_in.shape[0]
+    group = o_frame.shape[1]
+
+    barrier = pltpu.get_barrier_semaphore()
+    for k in range(1, n_dp):
+        pl.semaphore_signal(
+            barrier, inc=1, device_id=(lax.rem(me + k, n_dp), mp),
+            device_id_type=pl.DeviceIdType.MESH,
+        )
+    for k in range(1, n_mp):
+        pl.semaphore_signal(
+            barrier, inc=1, device_id=(me, lax.rem(mp + k, n_mp)),
+            device_id_type=pl.DeviceIdType.MESH,
+        )
+
+    def exchange(buf, s_sem, r_sem):
+        for k in range(1, n_dp):
+            remote(buf.at[me], buf.at[me], s_sem.at[k - 1], r_sem.at[k - 1],
+                   lax.rem(me + k, n_dp), mp).start()
+
+    def exchange_wait(buf, s_sem, r_sem):
+        for k in range(1, n_dp):
+            who = lax.rem(me + n_dp - k, n_dp)
+            c = remote(buf.at[who], buf.at[who], s_sem.at[k - 1], r_sem.at[k - 1], who, mp)
+            c.wait_recv()
+
+    def exchange_sent(buf, s_sem, r_sem):
+        for k in range(1, n_dp):
+            remote(buf.at[me], buf.at[me], s_sem.at[k - 1], r_sem.at[k - 1],
+                   lax.rem(me + k, n_dp), mp).wait_send()
+
+    def total_of(buf):
+        acc = buf[0]
+        for p in range(1, n_dp):
+            acc = acc + buf[p]
+        return acc
+
+    order = list(range(1, nz)) + [0]
+
+    def y_copy(k, s, r, s_sem, r_sem):
+        return remote(s.at[k], r.at[k], s_sem.at[k], r_sem.at[k], my_z * 2 + 1 - my_y, mp)
+
+    def z_copy(k, s, r, s_sem, r_sem):
+        return remote(s.at[k], r.at[k], s_sem.at[k], r_sem.at[k],
+                      lax.rem(my_z + k, nz) * 2 + my_y, mp)
+
+    def scatter_start(left, right, y_s, y_r, keep, ys_sem, yr_sem):
+        for k in order:
+            other = lax.rem(my_z + k, nz) * 2 + 1 - my_y
+            cols = pl.ds(pl.multiple_of(other * piece, piece), piece)
+            y_s[k] = dot(left[:, cols], right, TN).astype(jnp.bfloat16)
+            y_copy(k, y_s, y_r, ys_sem, yr_sem).start()
+        for k in order:
+            mine = lax.rem(my_z + k, nz) * 2 + my_y
+            cols = pl.ds(pl.multiple_of(mine * piece, piece), piece)
+            keep[k] = dot(left[:, cols], right, TN)
+
+    def scatter_mid(y_s, y_r, keep, z_s, z_r, ys_sem, yr_sem, zs_sem, zr_sem):
+        for k in order:
+            y_copy(k, y_s, y_r, ys_sem, yr_sem).wait_recv()
+            if k:
+                z_s[k] = (keep[k] + y_r[k].astype(jnp.float32)).astype(jnp.bfloat16)
+                z_copy(k, z_s, z_r, zs_sem, zr_sem).start()
+
+    def scatter_end(out, y_s, y_r, keep, z_s, z_r, ys_sem, yr_sem, zs_sem, zr_sem):
+        acc = keep[0] + y_r[0].astype(jnp.float32)
+        for k in range(1, nz):
+            z_copy(k, z_s, z_r, zs_sem, zr_sem).wait_recv()
+            acc = acc + z_r[k].astype(jnp.float32)
+        out[...] = acc
+        for k in range(nz):
+            y_copy(k, y_s, y_r, ys_sem, yr_sem).wait_send()
+            if k:
+                z_copy(k, z_s, z_r, zs_sem, zr_sem).wait_send()
+
+    my_live = counts[me] * BLOCK
+    total = counts[0]
+    for p in range(1, n_dp):
+        total = total + counts[p]
+    frame_total = (total * BLOCK).astype(jnp.float32)
+    r_id = lax.broadcasted_iota(jnp.int32, (rows, slots), 0)
+    s_id = lax.broadcasted_iota(jnp.int32, (rows, slots), 1)
+    target = s_id
+    end = 0
+    for u in range(lengths.shape[1] - 1):
+        end = end + lengths[0, u]
+        target = target + jnp.where(s_id >= end, GAP, 0)
+    place[...] = jnp.where((r_id == target) & (s_id < my_live), 1.0, 0.0).astype(jnp.bfloat16)
+    put = place[...]
+    live[...] = dot(put, jnp.ones((slots, chans), jnp.bfloat16))
+    fg[...] = dot(put, frames[...]).astype(jnp.bfloat16)
+    pre = dot(fg[...], proj[...])
+    v = pre[:, :chans]
+    g = jax.nn.sigmoid(pre[:, chans:])
+    val[...] = v
+    gate[...] = g
+    pad = jnp.zeros((GAP, chans), jnp.float32)
+    gpad[:GAP] = pad
+    gpad[GAP + rows:] = pad
+    cpad[:GAP] = pad
+    cpad[GAP + rows:] = pad
+    gpad[GAP:GAP + rows] = (v * g * live[...]).astype(jnp.bfloat16).astype(jnp.float32)
+
+    half = rows // 2
+    chunks = [(a, c) for a in range(0, rows, half) for c in range(0, chans, 128)]
+    for a, c in chunks:
+        acc = jnp.zeros((half, 128), jnp.float32)
+        for k in range(tap_count):
+            first = GAP + a + k - radius
+            acc = acc + taps[k:k + 1, c:c + 128] * gpad[first:first + half, c:c + 128]
+        conv[a:a + half, c:c + 128] = acc * live[a:a + half, c:c + 128]
+    cv = conv[...]
+    zero6 = jnp.zeros((6, chans), jnp.float32)
+    st1[me] = jnp.concatenate(
+        [jnp.sum(cv, axis=0, keepdims=True), jnp.sum(cv * cv, axis=0, keepdims=True), zero6], axis=0
+    )
+    pl.semaphore_wait(barrier, n_dp + n_mp - 2)
+    exchange(st1, st1_s, st1_r)
+
+    gg[...] = dot(put, grad_out[...]).astype(jnp.bfloat16)
+    gh[...] = dot(gg[...], proj_out[...])
+
+    exchange_wait(st1, st1_s, st1_r)
+    sums = total_of(st1)
+    mean = sums[0:1] / frame_total
+    inv = lax.rsqrt(sums[1:2] / frame_total - mean * mean + 1e-05)
+    normed = (conv[...] - mean) * inv
+    scaled = normed * gain[...] + shift[...]
+    sig = jax.nn.sigmoid(scaled)
+    hidden = (scaled * sig * live[...]).astype(jnp.bfloat16)
+    gscaled = gh[...] * live[...] * sig * (1.0 + scaled * (1.0 - sig))
+    gs[...] = gscaled
+    conv[...] = normed
+    st2[me] = jnp.concatenate(
+        [
+            jnp.sum(gscaled, axis=0, keepdims=True),
+            jnp.sum(gscaled * normed, axis=0, keepdims=True),
+            zero6,
+        ],
+        axis=0,
+    )
+    exchange(st2, st2_s, st2_r)
+    scatter_start(gg, hidden, oy_s, oy_r, okeep, oys_sem, oyr_sem)
+
+    exchange_wait(st2, st2_s, st2_r)
+    sums = total_of(st2)
+    o_shift[...] = sums[0:1]
+    o_gain[...] = sums[1:2]
+    cpad[GAP:GAP + rows] = (
+        live[...] * (gain[...] * inv)
+        * (gs[...] - sums[0:1] / frame_total - conv[...] * (sums[1:2] / frame_total))
+    )
+    for a, c in chunks:
+        acc = jnp.zeros((half, 128), jnp.float32)
+        for k in range(tap_count):
+            first = GAP + a + radius - k
+            acc = acc + taps[k:k + 1, c:c + 128] * cpad[first:first + half, c:c + 128]
+        acc = acc * live[a:a + half, c:c + 128]
+        gt = gate[a:a + half, c:c + 128]
+        gval = acc * gt
+        gp[a:a + half, c:c + 128] = gval.astype(jnp.bfloat16)
+        ggate = gval * val[a:a + half, c:c + 128] * (1.0 - gt)
+        gp[a:a + half, chans + c:chans + c + 128] = ggate.astype(jnp.bfloat16)
+
+    scatter_start(fg, gp[...], iy_s, iy_r, ikeep, iys_sem, iyr_sem)
+    scatter_mid(oy_s, oy_r, okeep, oz_s, oz_r, oys_sem, oyr_sem, ozs_sem, ozr_sem)
+
+    def f_copy(k):
+        return remote(f_s.at[k], f_r.at[k], fs_sem.at[k], fr_sem.at[k],
+                      me, lax.rem(mp + k, n_mp))
+
+    back = dot(place[...], gp[...], TN).astype(jnp.bfloat16)
+    for k in list(range(1, n_mp)) + [0]:
+        peer = lax.rem(mp + k, n_mp)
+        part = proj[pl.ds(pl.multiple_of(peer * group, group), group), :]
+        f_s[k] = dot(back, part, NT).astype(jnp.bfloat16)
+        if k:
+            f_copy(k).start()
+
+    scatter_mid(iy_s, iy_r, ikeep, iz_s, iz_r, iys_sem, iyr_sem, izs_sem, izr_sem)
+
+    per = -(-tap_count // n_dp)
+    d_s[...] = jnp.zeros(d_s.shape, jnp.float32)
+    for c in range(0, chans, 128):
+        grad_c = cpad[GAP:GAP + rows, c:c + 128]
+        for k in range(tap_count):
+            first = GAP + k - radius
+            d_s[k // per, k % per:k % per + 1, c:c + 128] = jnp.sum(
+                grad_c * gpad[first:first + rows, c:c + 128], axis=0, keepdims=True
+            )
+
+    def d_copy(k):
+        peer = lax.rem(me + k, n_dp)
+        return remote(d_s.at[peer], d_r.at[k], ds_sem.at[k], dr_sem.at[k], peer, mp)
+
+    for k in range(1, n_dp):
+        d_copy(k).start()
+    acc = d_s[me]
+    for k in range(1, n_dp):
+        d_copy(k).wait_recv()
+        acc = acc + d_r[k]
+    e_r[me] = acc
+    exchange(e_r, es_sem, er_sem)
+
+    scatter_end(o_out, oy_s, oy_r, okeep, oz_s, oz_r, oys_sem, oyr_sem, ozs_sem, ozr_sem)
+    facc = f_s[0].astype(jnp.float32)
+    for k in range(1, n_mp):
+        f_copy(k).wait_recv()
+        facc = facc + f_r[k].astype(jnp.float32)
+    o_frame[...] = facc.astype(jnp.bfloat16)
+    exchange_wait(e_r, es_sem, er_sem)
+    for p in range(n_dp):
+        many = min(per, tap_count - p * per)
+        if many > 0:
+            o_depth[p * per:p * per + many] = e_r[p, :many]
+    scatter_end(o_in, iy_s, iy_r, ikeep, iz_s, iz_r, iys_sem, iyr_sem, izs_sem, izr_sem)
+    exchange_sent(st1, st1_s, st1_r)
+    exchange_sent(st2, st2_s, st2_r)
+    exchange_sent(e_r, es_sem, er_sem)
+    for k in range(1, n_mp):
+        f_copy(k).wait_send()
+    for k in range(1, n_dp):
+        d_copy(k).wait_send()
+
+
+def fused_shards(
+    frames, proj_in, depthwise, bn_gain, bn_shift, proj_out, grad_out, counts, lengths
+):
+    n_dp, n_mp = lax.axis_size("dp"), lax.axis_size("mp")
+    slots, width = frames.shape
+    chans = proj_in.shape[2]
+    tap_count = depthwise.shape[0]
+    rows = slots + GAP * (lengths.shape[1] - 1)
+    piece = width // n_dp
+    group = width // n_mp
+    nz = n_dp // 2
+    per8 = -(-(-(-tap_count // n_dp)) // 8) * 8
+    f32, bf16 = jnp.float32, jnp.bfloat16
+    vm, dma = pltpu.VMEM, pltpu.SemaphoreType.DMA
+    sem_pair = [dma((n_dp,)), dma((n_dp,))]
+
+    def ring(wide):
+        shape = (nz, piece, wide)
+        return [vm(shape, bf16), vm(shape, bf16), vm(shape, f32), vm(shape, bf16),
+                vm(shape, bf16)] + [dma((nz,))] * 4
+
+    full = vm((rows, chans), f32)
+    padded = vm((rows + 2 * GAP, chans), f32)
+    in_vmem = pl.BlockSpec(memory_space=pltpu.VMEM)
+    in_smem = pl.BlockSpec(memory_space=pltpu.SMEM)
+    frame_grad, in_flat, out_grad, depth_grad, gain_grad, shift_grad = pl.pallas_call(
+        functools.partial(fused, n_dp, n_mp),
+        out_shape=[
+            jax.ShapeDtypeStruct((slots, group), bf16),
+            jax.ShapeDtypeStruct((piece, 2 * chans), f32),
+            jax.ShapeDtypeStruct((piece, chans), f32),
+            jax.ShapeDtypeStruct((tap_count, chans), f32),
+            jax.ShapeDtypeStruct((1, chans), f32),
+            jax.ShapeDtypeStruct((1, chans), f32),
+        ],
+        in_specs=[in_vmem] * 7 + [in_smem] * 2,
+        out_specs=[in_vmem] * 6,
+        scratch_shapes=[
+            vm((rows, slots), bf16), full, vm((rows, width), bf16), vm((rows, width), bf16),
+            padded, padded, full, full, full, full, full, vm((rows, 2 * chans), bf16),
+            vm((n_dp, 8, chans), f32), *sem_pair, vm((n_dp, 8, chans), f32), *sem_pair,
+            *ring(chans), *ring(2 * chans),
+            vm((n_mp, slots, group), bf16), vm((n_mp, slots, group), bf16),
+            dma((n_mp,)), dma((n_mp,)),
+            vm((n_dp, per8, chans), f32), vm((n_dp, per8, chans), f32), *sem_pair,
+            vm((n_dp, per8, chans), f32), *sem_pair,
+        ],
+        compiler_params=pltpu.CompilerParams(
+            collective_id=0, has_side_effects=True, vmem_limit_bytes=48 * 1024 * 1024
+        ),
+    )(
+        frames, proj_in.reshape(width, 2 * chans), depthwise, bn_gain[None], bn_shift[None],
+        proj_out, grad_out, counts, lengths,
+    )
+    return (
+        frame_grad, in_flat.reshape(piece, 2, chans), out_grad, depth_grad,
+        gain_grad.reshape(chans), shift_grad.reshape(chans),
+    )
+
+
+def pick(*args):
+    n_dp = lax.axis_size("dp")
+    frames, proj_in, taps = args[0], args[1], args[2]
+    fits = (
+        n_dp % 2 == 0 and n_dp <= 16 and frames.shape[1] % (128 * n_dp) == 0
+        and proj_in.shape[2] % 128 == 0 and frames.shape[0] % 16 == 0
+        and taps.shape[0] // 2 <= GAP
+    )
+    return (fused_shards if fits else shards)(*args)
+
+
 def solution(mesh):
     placed = (
         P("dp", None),
@@ -125,7 +465,7 @@
         P("dp", None),
     )
     return jax.shard_map(
-        shards,
+        pick,
         mesh=mesh,
         in_specs=placed,
         out_specs=(

time: 210 us -> 49.2 us (0.23)
  blocking collectives: 77.3 us -> 0 us
  waiting for transfers between devices: 47.4 us -> 0 us
  Pallas kernels: 0 us -> 42.2 us
  local copies, waits for them, and re-layouts: 36.3 us -> 6.13 us
  other arithmetic: 24.7 us -> 0 us
  between operations: 16.7 us -> 0.75 us
  matrix products: 6.97 us -> 0 us
    psum x3 -> x0, blocking collectives: 77.3 us -> none  [the longest x1 36.4 us: shards(): depth_grad = lax.psum(jnp.stack(depth_rows), 'dp')]
    reduce_scatter x2 -> x0, waiting for transfers between devices: 47.3 us -> none  [the longest x1 26.7 us: shards(): lax.psum_scatter(jnp.concatenate([lax.dot_general(frames, grad_flat, (((0...]
    pallas_call x0 -> x1, Pallas kernels: none -> 42.2 us  [fused_shards(): pl.pallas_call(functools.partial(fused, n_dp, n_mp), out_shape=[jax.Shape...]
    slice x49 -> x0, local copies, waits for them, and re-layouts: 27.3 us -> none  [the longest x29 21 us: time_shift(): return jnp.concatenate([pad_part, values[:offset]], axis=0)]
    reduce_sum x7 -> x0, other arithmetic: 16.6 us -> none  [the longest x4 9.01 us: shards(): jnp.sum(grad_conv * tap_term(glu_float, owner_id, live_col, tap_index - r...]
    dot_general x5 -> x0, matrix products: 6.97 us -> none  [the longest x1 2.32 us: shards(): jnp.dot(grad_out, proj_out, preferred_element_type=jnp.float32) * live_col]
    another operation x3 -> x0, other arithmetic: 4.35 us -> none
    another operation x1 -> x0, local copies, waits for them, and re-layouts: 2.86 us -> none  [shards(): depth_grad = lax.psum(jnp.stack(depth_rows), 'dp')]
  transfers between devices with their start and end apart: 2 -> 0, of which waited for: 2 -> 0; matrix products, arithmetic and copies ran while one was open for 7% -> 0% of each run, Pallas kernels for 0% -> 0%
where the time goes in v1:
time: 49.2 us; the launch traced here: 49.1 us
  Pallas kernels  42.2 us (86%)
  local copies, waits for them, and re-layouts  6.13 us (12%)
  between operations  0.75 us (2%)
    pallas_call x1, Pallas kernels, fused_shards(): pl.pallas_call(functools.partial(fused, n_dp, n_mp), out_shape=[jax.Shape...  42.2 us
    unnamed x22, local copies, waits for them, and re-layouts  5.26 us

profile of v1, /device:TPU:0, one launch (start us, length us, event | category | flops | bytes accessed | tf_op | source)
XLA Modules:
  0.0 49.1 jit_solution(15187098179386488646)
XLA Ops:
  0.6 0.0 copy-start
  0.6 0.0 copy-start.1
  0.7 0.0 copy-start.2
  0.7 0.0 copy-start.3
  0.7 0.0 copy-start.5
  0.7 0.0 copy-start.7
  0.7 1.6 %copy.15 = bf16[128,8,2,256]{3,1,2,0:T(8,128)(2,1)S(1)} copy(bf16[128,8,2,256]{3,2,1,0:T(2,128)(2,1)} %bitcast.11) | data formatting | bytes 2097152
  2.3 0.0 copy-start.4
  2.3 0.0 copy-start.6
  2.3 0.0 copy-done
  2.3 0.0 copy-done.1
  2.3 0.0 copy-done.2
  2.3 0.0 copy-done.3
  2.3 0.0 copy-done.5
  2.3 0.0 copy-done.7
  2.3 0.6 %copy-done.4 = f32[256]{0:T(256)S(1)} copy-done((f32[256]{0:T(256)S(1)}, f32[256]{0:T(256)}, u32[]{:S(2)}) %copy-start.4) | copy-done | bytes 1048
  3.0 0.0 copy-done.6
  3.0 42.2 %shard_map.136 = (bf16[256,256]{1,0:T(8,128)(2,1)S(1)}, f32[128,512]{1,0:T(8,128)S(1)}, f32[128,256]{1,0:T(8,128)S(1)}, f32[31,256]{1,0:T(8,128)S(1)}, f32[1,256]{1,0:T(1,128)S(1)}, /*index=5*/f32[1,256]{1,0:T(1,128)S(1)}) custom-call(bf16[256,1024]{1,0:T(8,128)(2,1)S(1)} %copy-done, bf16[1024,512]{1,0:T(8,128)(2,1)S(1)} %bitcast.6, ...), custom_call_target="tpu_custom_call" | custom-call | tf_op jit(solution)/shard_map/pallas_call | solution.py:409
  45.1 0.9 %reshape.25 = f32[128,2,256]{2,1,0:T(2,128)} reshape(f32[128,512]{1,0:T(8,128)S(1)} %get-tuple-element.13) | data formatting | bytes 524288 | tf_op jit(solution)/shard_map/reshape | solution.py:439
  46.0 0.7 %copy.21 = bf16[256,256]{1,0:T(8,128)(2,1)} copy(bf16[256,256]{1,0:T(8,128)(2,1)S(1)} %get-tuple-element.24) | data formatting | bytes 262144
  46.7 0.7 %copy.22 = f32[128,256]{1,0:T(8,128)} copy(f32[128,256]{1,0:T(8,128)S(1)} %get-tuple-element.26) | data formatting | bytes 262144
  47.3 0.6 %copy.23 = f32[31,256]{1,0:T(8,128)} copy(f32[31,256]{1,0:T(8,128)S(1)} %get-tuple-element.27) | data formatting | bytes 63488
  47.9 0.6 %copy.24 = f32[256]{0:T(256)} copy(f32[256]{0:T(256)S(1)} %bitcast.10) | data formatting | bytes 2048
  48.5 0.6 %copy.25 = f32[256]{0:T(256)} copy(f32[256]{0:T(256)S(1)} %bitcast.9) | data formatting | bytes 2048
Async XLA Ops:
  0.6 1.6 %copy-start = (bf16[256,1024]{1,0:T(8,128)(2,1)S(1)}, bf16[256,1024]{1,0:T(8,128)(2,1)}, u32[]{:S(2)}) copy-start(bf16[256,1024]{1,0:T(8,128)(2,1)} %frames.1) | copy-start | bytes 1572868
  0.6 1.6 %copy-start.1 = (bf16[1024,256]{1,0:T(8,128)(2,1)S(1)}, bf16[1024,256]{1,0:T(8,128)(2,1)}, u32[]{:S(2)}) copy-start(bf16[1024,256]{1,0:T(8,128)(2,1)} %proj_out.1) | copy-start | bytes 1572868
  0.7 1.7 %copy-start.2 = (bf16[256,1024]{1,0:T(8,128)(2,1)S(1)}, bf16[256,1024]{1,0:T(8,128)(2,1)}, u32[]{:S(2)}) copy-start(bf16[256,1024]{1,0:T(8,128)(2,1)} %grad_out.1) | copy-start | bytes 1572868
  0.7 1.6 %copy-start.3 = (f32[31,256]{1,0:T(8,128)S(1)}, f32[31,256]{1,0:T(8,128)}, u32[]{:S(2)}) copy-start(f32[31,256]{1,0:T(8,128)} %taps.1) | copy-start | bytes 95236
  0.7 1.6 %copy-start.5 = (f32[256]{0:T(256)S(1)}, f32[256]{0:T(256)}, u32[]{:S(2)}) copy-start(f32[256]{0:T(256)} %param.13) | copy-start | bytes 3076
  0.7 1.6 %copy-start.7 = (s32[1,2]{1,0:T(1,128)S(1)}, s32[1,2]{1,0:T(1,128)}, u32[]{:S(2)}) copy-start(s32[1,2]{1,0:T(1,128)} %lengths.1) | copy-start | bytes 28
  2.3 0.7 %copy-start.4 = (f32[256]{0:T(256)S(1)}, f32[256]{0:T(256)}, u32[]{:S(2)}) copy-start(f32[256]{0:T(256)} %param.12) | copy-start | bytes 3076
  2.3 0.7 %copy-start.6 = (s32[8]{0:T(128)S(1)}, s32[8]{0:T(128)}, u32[]{:S(2)}) copy-start(s32[8]{0:T(128)} %counts.1) | copy-start | bytes 100

commit v2 on v1

--- a/solution.py
+++ b/solution.py
@@ -142,11 +142,12 @@
     o_frame, o_in, o_out, o_depth, o_gain, o_shift,
     place, live, fg, gg, gpad, cpad, val, gate, conv, gh, gs, gp,
     st1, st1_s, st1_r, st2, st2_s, st2_r,
-    oy_s, oy_r, okeep, oz_s, oz_r, oys_sem, oyr_sem, ozs_sem, ozr_sem,
-    iy_s, iy_r, ikeep, iz_s, iz_r, iys_sem, iyr_sem, izs_sem, izr_sem,
     f_s, f_r, fs_sem, fr_sem,
     d_s, d_r, ds_sem, dr_sem, e_r, es_sem, er_sem,
+    *ring_refs,
 ):
+    out_ring = ring_refs[:9]
+    in_rings = [ring_refs[i:i + 9] for i in range(9, len(ring_refs), 9)]
     rows, chans = conv.shape
     slots = frames.shape[0]
     tap_count = taps.shape[0]
@@ -202,30 +203,37 @@
         return remote(s.at[k], r.at[k], s_sem.at[k], r_sem.at[k],
                       lax.rem(my_z + k, nz) * 2 + my_y, mp)
 
-    def scatter_start(left, right, y_s, y_r, keep, ys_sem, yr_sem):
+    def scatter_send(ring, left, right):
+        y_s, y_r, _, _, _, ys_sem, yr_sem, _, _ = ring
         for k in order:
             other = lax.rem(my_z + k, nz) * 2 + 1 - my_y
             cols = pl.ds(pl.multiple_of(other * piece, piece), piece)
             y_s[k] = dot(left[:, cols], right, TN).astype(jnp.bfloat16)
             y_copy(k, y_s, y_r, ys_sem, yr_sem).start()
+
+    def scatter_keep(ring, left, right):
         for k in order:
             mine = lax.rem(my_z + k, nz) * 2 + my_y
             cols = pl.ds(pl.multiple_of(mine * piece, piece), piece)
-            keep[k] = dot(left[:, cols], right, TN)
-
-    def scatter_mid(y_s, y_r, keep, z_s, z_r, ys_sem, yr_sem, zs_sem, zr_sem):
-        for k in order:
-            y_copy(k, y_s, y_r, ys_sem, yr_sem).wait_recv()
-            if k:
-                z_s[k] = (keep[k] + y_r[k].astype(jnp.float32)).astype(jnp.bfloat16)
-                z_copy(k, z_s, z_r, zs_sem, zr_sem).start()
-
-    def scatter_end(out, y_s, y_r, keep, z_s, z_r, ys_sem, yr_sem, zs_sem, zr_sem):
+            ring[2][k] = dot(left[:, cols], right, TN)
+
+    def scatter_mid(ring, k):
+        y_s, y_r, keep, z_s, z_r, ys_sem, yr_sem, zs_sem, zr_sem = ring
+        y_copy(k, y_s, y_r, ys_sem, yr_sem).wait_recv()
+        if k:
+            z_s[k] = (keep[k] + y_r[k].astype(jnp.float32)).astype(jnp.bfloat16)
+            z_copy(k, z_s, z_r, zs_sem, zr_sem).start()
+
+    def scatter_end(ring):
+        y_s, y_r, keep, z_s, z_r, ys_sem, yr_sem, zs_sem, zr_sem = ring
         acc = keep[0] + y_r[0].astype(jnp.float32)
         for k in range(1, nz):
             z_copy(k, z_s, z_r, zs_sem, zr_sem).wait_recv()
             acc = acc + z_r[k].astype(jnp.float32)
-        out[...] = acc
+        return acc
+
+    def scatter_sent(ring):
+        y_s, y_r, keep, z_s, z_r, ys_sem, yr_sem, zs_sem, zr_sem = ring
         for k in range(nz):
             y_copy(k, y_s, y_r, ys_sem, yr_sem).wait_send()
             if k:
@@ -298,7 +306,8 @@
         axis=0,
     )
     exchange(st2, st2_s, st2_r)
-    scatter_start(gg, hidden, oy_s, oy_r, okeep, oys_sem, oyr_sem)
+    scatter_send(out_ring, gg, hidden)
+    scatter_keep(out_ring, gg, hidden)
 
     exchange_wait(st2, st2_s, st2_r)
     sums = total_of(st2)
@@ -308,25 +317,54 @@
         live[...] * (gain[...] * inv)
         * (gs[...] - sums[0:1] / frame_total - conv[...] * (sums[1:2] / frame_total))
     )
-    for a, c in chunks:
-        acc = jnp.zeros((half, 128), jnp.float32)
-        for k in range(tap_count):
-            first = GAP + a + radius - k
-            acc = acc + taps[k:k + 1, c:c + 128] * cpad[first:first + half, c:c + 128]
-        acc = acc * live[a:a + half, c:c + 128]
-        gt = gate[a:a + half, c:c + 128]
-        gval = acc * gt
-        gp[a:a + half, c:c + 128] = gval.astype(jnp.bfloat16)
-        ggate = gval * val[a:a + half, c:c + 128] * (1.0 - gt)
-        gp[a:a + half, chans + c:chans + c + 128] = ggate.astype(jnp.bfloat16)
-
-    scatter_start(fg, gp[...], iy_s, iy_r, ikeep, iys_sem, iyr_sem)
-    scatter_mid(oy_s, oy_r, okeep, oz_s, oz_r, oys_sem, oyr_sem, ozs_sem, ozr_sem)
+    out_steps = list(order)
+
+    def half_grad(i):
+        return jnp.concatenate(
+            [gp[:, i * 128:i * 128 + 128], gp[:, chans + i * 128:chans + i * 128 + 128]], axis=1
+        )
+
+    for i, ring in enumerate(in_rings):
+        c = i * 128
+        for a in range(0, rows, half):
+            acc = jnp.zeros((half, 128), jnp.float32)
+            for k in range(tap_count):
+                first = GAP + a + radius - k
+                acc = acc + taps[k:k + 1, c:c + 128] * cpad[first:first + half, c:c + 128]
+            acc = acc * live[a:a + half, c:c + 128]
+            gt = gate[a:a + half, c:c + 128]
+            gval = acc * gt
+            gp[a:a + half, c:c + 128] = gval.astype(jnp.bfloat16)
+            ggate = gval * val[a:a + half, c:c + 128] * (1.0 - gt)
+            gp[a:a + half, chans + c:chans + c + 128] = ggate.astype(jnp.bfloat16)
+            if out_steps:
+                scatter_mid(out_ring, out_steps.pop(0))
+        scatter_send(ring, fg, half_grad(i))
+    for k in out_steps:
+        scatter_mid(out_ring, k)
 
     def f_copy(k):
         return remote(f_s.at[k], f_r.at[k], fs_sem.at[k], fr_sem.at[k],
                       me, lax.rem(mp + k, n_mp))
 
+    per = -(-tap_count // n_dp)
+
+    def tap_sums(c):
+        grad_c = cpad[GAP:GAP + rows, c:c + 128]
+        for k in range(tap_count):
+            first = GAP + k - radius
+            d_s[k // per, k % per:k % per + 1, c:c + 128] = jnp.sum(
+                grad_c * gpad[first:first + rows, c:c + 128], axis=0, keepdims=True
+            )
+
+    def d_copy(k):
+        peer = lax.rem(me + k, n_dp)
+        return remote(d_s.at[peer], d_r.at[k], ds_sem.at[k], dr_sem.at[k], peer, mp)
+
+    d_s[...] = jnp.zeros(d_s.shape, jnp.float32)
+    scatter_keep(in_rings[0], fg, half_grad(0))
+    for k in order[:-1]:
+        scatter_mid(in_rings[0], k)
     back = dot(place[...], gp[...], TN).astype(jnp.bfloat16)
     for k in list(range(1, n_mp)) + [0]:
         peer = lax.rem(mp + k, n_mp)
@@ -334,25 +372,18 @@
         f_s[k] = dot(back, part, NT).astype(jnp.bfloat16)
         if k:
             f_copy(k).start()
-
-    scatter_mid(iy_s, iy_r, ikeep, iz_s, iz_r, iys_sem, iyr_sem, izs_sem, izr_sem)
-
-    per = -(-tap_count // n_dp)
-    d_s[...] = jnp.zeros(d_s.shape, jnp.float32)
+    scatter_mid(in_rings[0], 0)
+    for i in range(1, len(in_rings)):
+        scatter_keep(in_rings[i], fg, half_grad(i))
+    steps = [(ring, k) for ring in in_rings[1:] for k in order]
     for c in range(0, chans, 128):
-        grad_c = cpad[GAP:GAP + rows, c:c + 128]
-        for k in range(tap_count):
-            first = GAP + k - radius
-            d_s[k // per, k % per:k % per + 1, c:c + 128] = jnp.sum(
-                grad_c * gpad[first:first + rows, c:c + 128], axis=0, keepdims=True
-            )
-
-    def d_copy(k):
-        peer = lax.rem(me + k, n_dp)
-        return remote(d_s.at[peer], d_r.at[k], ds_sem.at[k], dr_sem.at[k], peer, mp)
-
+        tap_sums(c)
+        if steps:
+            scatter_mid(*steps.pop(0))
     for k in range(1, n_dp):
         d_copy(k).start()
+    for ring, k in steps:
+        scatter_mid(ring, k)
     acc = d_s[me]
     for k in range(1, n_dp):
         d_copy(k).wait_recv()
@@ -360,18 +391,23 @@
     e_r[me] = acc
     exchange(e_r, es_sem, er_sem)
 
-    scatter_end(o_out, oy_s, oy_r, okeep, oz_s, oz_r, oys_sem, oyr_sem, ozs_sem, ozr_sem)
+    o_out[...] = scatter_end(out_ring)
     facc = f_s[0].astype(jnp.float32)
     for k in range(1, n_mp):
         f_copy(k).wait_recv()
         facc = facc + f_r[k].astype(jnp.float32)
     o_frame[...] = facc.astype(jnp.bfloat16)
+    for i, ring in enumerate(in_rings):
+        both = scatter_end(ring)
+        o_in[:, i * 128:i * 128 + 128] = both[:, :128]
+        o_in[:, chans + i * 128:chans + i * 128 + 128] = both[:, 128:]
     exchange_wait(e_r, es_sem, er_sem)
     for p in range(n_dp):
         many = min(per, tap_count - p * per)
         if many > 0:
             o_depth[p * per:p * per + many] = e_r[p, :many]
-    scatter_end(o_in, iy_s, iy_r, ikeep, iz_s, iz_r, iys_sem, iyr_sem, izs_sem, izr_sem)
+    for ring in [out_ring] + in_rings:
+        scatter_sent(ring)
     exchange_sent(st1, st1_s, st1_r)
     exchange_sent(st2, st2_s, st2_r)
     exchange_sent(e_r, es_sem, er_sem)
@@ -379,6 +415,12 @@
         f_copy(k).wait_send()
     for k in range(1, n_dp):
         d_copy(k).wait_send()
+
+
+def hand_on(*refs):
+    half = len(refs) // 2
+    for src, dst in zip(refs[:half], refs[half:]):
+        dst[...] = src[...]
 
 
 def fused_shards(
@@ -422,11 +464,11 @@
             vm((rows, slots), bf16), full, vm((rows, width), bf16), vm((rows, width), bf16),
             padded, padded, full, full, full, full, full, vm((rows, 2 * chans), bf16),
             vm((n_dp, 8, chans), f32), *sem_pair, vm((n_dp, 8, chans), f32), *sem_pair,
-            *ring(chans), *ring(2 * chans),
             vm((n_mp, slots, group), bf16), vm((n_mp, slots, group), bf16),
             dma((n_mp,)), dma((n_mp,)),
             vm((n_dp, per8, chans), f32), vm((n_dp, per8, chans), f32), *sem_pair,
             vm((n_dp, per8, chans), f32), *sem_pair,
+            *ring(chans), *(ref for _ in range(chans // 128) for ref in ring(256)),
         ],
         compiler_params=pltpu.CompilerParams(
             collective_id=0, has_side_effects=True, vmem_limit_bytes=48 * 1024 * 1024
@@ -435,6 +477,15 @@
         frames, proj_in.reshape(width, 2 * chans), depthwise, bn_gain[None], bn_shift[None],
         proj_out, grad_out, counts, lengths,
     )
+    frame_grad, out_grad, depth_grad, gain_grad, shift_grad = pl.pallas_call(
+        hand_on,
+        out_shape=[
+            jax.ShapeDtypeStruct(x.shape, x.dtype)
+            for x in (frame_grad, out_grad, depth_grad, gain_grad, shift_grad)
+        ],
+        in_specs=[in_vmem] * 5,
+        out_specs=[in_vmem] * 5,
+    )(frame_grad, out_grad, depth_grad, gain_grad, shift_grad)
     return (
         frame_grad, in_flat.reshape(piece, 2, chans), out_grad, depth_grad,
         gain_grad.reshape(chans), shift_grad.reshape(chans),

time: 49.2 us -> 48.8 us (level)
  local copies, waits for them, and re-layouts: 6.13 us -> 5.57 us
    pallas_call x0 -> x1, Pallas kernels: none -> 1.69 us  [fused_shards(): pl.pallas_call(hand_on, out_shape=[jax.ShapeDtypeStruct(x.shape, x.dtype)...]
    pallas_call x1, Pallas kernels: 42.2 us -> 40.6 us  [fused_shards(): pl.pallas_call(functools.partial(fused, n_dp, n_mp), out_shape=[jax.Shape...]
    unnamed x22 -> x27, local copies, waits for them, and re-layouts: 5.26 us -> 4.71 us
where the time goes in v2:
time: 48.8 us; the launch traced here: 48.6 us
  Pallas kernels  42.3 us (87%)
  local copies, waits for them, and re-layouts  5.57 us (11%)
  between operations  0.77 us (2%)
    pallas_call x1, Pallas kernels, fused_shards(): pl.pallas_call(functools.partial(fused, n_dp, n_mp), out_shape=[jax.Shape...  40.6 us
    unnamed x27, local copies, waits for them, and re-layouts  4.71 us
    pallas_call x1, Pallas kernels, fused_shards(): pl.pallas_call(hand_on, out_shape=[jax.ShapeDtypeStruct(x.shape, x.dtype)...  1.69 us

profile of v2, /device:TPU:0, one launch (start us, length us, event | category | flops | bytes accessed | tf_op | source)
XLA Modules:
  0.0 48.6 jit_solution(13103511161169807121)
XLA Ops:
  0.6 0.0 copy-start
  0.6 0.0 copy-start.1
  0.7 0.0 copy-start.2
  0.7 0.0 copy-start.5
  0.7 0.0 copy-start.8
  0.7 0.0 copy-start.12
  0.7 1.6 %copy.15 = bf16[128,8,2,256]{3,1,2,0:T(8,128)(2,1)S(1)} copy(bf16[128,8,2,256]{3,2,1,0:T(2,128)(2,1)} %bitcast.9) | data formatting | bytes 2097152
  2.3 0.0 copy-start.7
  2.3 0.0 copy-start.11
  2.3 0.0 copy-done
  2.3 0.0 copy-done.1
  2.3 0.0 copy-done.2
  2.3 0.0 copy-done.5
  2.3 0.0 copy-done.8
  2.3 0.0 copy-done.12
  2.3 0.6 %copy-done.7 = f32[256]{0:T(256)S(1)} copy-done((f32[256]{0:T(256)S(1)}, f32[256]{0:T(256)}, u32[]{:S(2)}) %copy-start.7) | copy-done | bytes 1048
  3.0 0.0 copy-done.11
  3.0 40.6 %shard_map.136 = (bf16[256,256]{1,0:T(8,128)(2,1)S(1)}, f32[128,512]{1,0:T(8,128)S(1)}, f32[128,256]{1,0:T(8,128)S(1)}, f32[31,256]{1,0:T(8,128)S(1)}, f32[1,256]{1,0:T(1,128)S(1)}, /*index=5*/f32[1,256]{1,0:T(1,128)S(1)}) custom-call(bf16[256,1024]{1,0:T(8,128)(2,1)S(1)} %copy-done, bf16[1024,512]{1,0:T(8,128)(2,1)S(1)} %bitcast.6, ...), custom_call_target="tpu_custom_call" | custom-call | tf_op jit(solution)/shard_map/pallas_call | solution.py:451
  43.6 0.0 copy-start.3
  43.6 0.6 %copy-done.3 = bf16[256,256]{1,0:T(8,128)(2,1)} copy-done((bf16[256,256]{1,0:T(8,128)(2,1)}, bf16[256,256]{1,0:T(8,128)(2,1)S(1)}, u32[]{:S(2)}) %copy-start.3) | copy-done | bytes 131096
  44.2 0.0 copy-start.4
  44.2 0.6 %copy-done.4 = f32[128,256]{1,0:T(8,128)} copy-done((f32[128,256]{1,0:T(8,128)}, f32[128,256]{1,0:T(8,128)S(1)}, u32[]{:S(2)}) %copy-start.4) | copy-done | bytes 131096
  44.9 0.0 copy-start.6
  44.9 0.6 %copy-done.6 = f32[31,256]{1,0:T(8,128)} copy-done((f32[31,256]{1,0:T(8,128)}, f32[31,256]{1,0:T(8,128)S(1)}, u32[]{:S(2)}) %copy-start.6) | copy-done | bytes 31768
  45.5 0.0 copy-start.9
  45.5 0.0 copy-start.10
  45.5 0.5 %copy-done.9 = f32[1,256]{1,0:T(1,128)} copy-done((f32[1,256]{1,0:T(1,128)}, f32[1,256]{1,0:T(1,128)S(1)}, u32[]{:S(2)}) %copy-start.9) | copy-done | bytes 1048
  46.0 0.1 copy-done.10
  46.1 1.7 %shard_map.137 = (bf16[256,256]{1,0:T(8,128)(2,1)}, f32[128,256]{1,0:T(8,128)}, f32[31,256]{1,0:T(8,128)}, f32[1,256]{1,0:T(1,128)}, f32[1,256]{1,0:T(1,128)}) custom-call(bf16[256,256]{1,0:T(8,128)(2,1)} %copy-done.3, f32[128,256]{1,0:T(8,128)} %copy-done.4, f32[31,256]{1,0:T(8,128)} %copy-done.6, f32[1,256]{1,0:T(1,128)} %copy-done.9, f32[1,256]{1,0:T(1,128)} %copy-done.10), custom_call_target="tpu_custom_call" | custom-call | tf_op jit(solution)/shard_map/pallas_call | solution.py:480
  47.8 0.9 %reshape.25 = f32[128,2,256]{2,1,0:T(2,128)} reshape(f32[128,512]{1,0:T(8,128)S(1)} %get-tuple-element.23) | data formatting | bytes 524288 | tf_op jit(solution)/shard_map/reshape | solution.py:490
Async XLA Ops:
  0.6 1.6 %copy-start = (bf16[256,1024]{1,0:T(8,128)(2,1)S(1)}, bf16[256,1024]{1,0:T(8,128)(2,1)}, u32[]{:S(2)}) copy-start(bf16[256,1024]{1,0:T(8,128)(2,1)} %frames.1) | copy-start | bytes 1572868
  0.6 1.6 %copy-start.1 = (bf16[1024,256]{1,0:T(8,128)(2,1)S(1)}, bf16[1024,256]{1,0:T(8,128)(2,1)}, u32[]{:S(2)}) copy-start(bf16[1024,256]{1,0:T(8,128)(2,1)} %proj_out.1) | copy-start | bytes 1572868
  0.7 1.7 %copy-start.2 = (bf16[256,1024]{1,0:T(8,128)(2,1)S(1)}, bf16[256,1024]{1,0:T(8,128)(2,1)}, u32[]{:S(2)}) copy-start(bf16[256,1024]{1,0:T(8,128)(2,1)} %grad_out.1) | copy-start | bytes 1572868
  0.7 1.6 %copy-start.5 = (f32[31,256]{1,0:T(8,128)S(1)}, f32[31,256]{1,0:T(8,128)}, u32[]{:S(2)}) copy-start(f32[31,256]{1,0:T(8,128)} %taps.1) | copy-start | bytes 95236
  0.7 1.6 %copy-start.8 = (f32[256]{0:T(256)S(1)}, f32[256]{0:T(256)}, u32[]{:S(2)}) copy-start(f32[256]{0:T(256)} %param.13) | copy-start | bytes 3076
  0.7 1.6 %copy-start.12 = (s32[1,2]{1,0:T(1,128)S(1)}, s32[1,2]{1,0:T(1,128)}, u32[]{:S(2)}) copy-start(s32[1,2]{1,0:T(1,128)} %lengths.1) | copy-start | bytes 28
  2.3 0.7 %copy-start.7 = (f32[256]{0:T(256)S(1)}, f32[256]{0:T(256)}, u32[]{:S(2)}) copy-start(f32[256]{0:T(256)} %param.12) | copy-start | bytes 3076
  2.3 0.7 %copy-start.11 = (s32[8]{0:T(128)S(1)}, s32[8]{0:T(128)}, u32[]{:S(2)}) copy-start(s32[8]{0:T(128)} %counts.1) | copy-start | bytes 100
  43.6 0.7 %copy-start.3 = (bf16[256,256]{1,0:T(8,128)(2,1)}, bf16[256,256]{1,0:T(8,128)(2,1)S(1)}, u32[]{:S(2)}) copy-start(bf16[256,256]{1,0:T(8,128)(2,1)S(1)} %get-tuple-element.17.refs_0_) | copy-start | bytes 393220
  44.2 0.6 %copy-start.4 = (f32[128,256]{1,0:T(8,128)}, f32[128,256]{1,0:T(8,128)S(1)}, u32[]{:S(2)}) copy-start(f32[128,256]{1,0:T(8,128)S(1)} %get-tuple-element.18.refs_1_) | copy-start | bytes 393220
  44.9 0.6 %copy-start.6 = (f32[31,256]{1,0:T(8,128)}, f32[31,256]{1,0:T(8,128)S(1)}, u32[]{:S(2)}) copy-start(f32[31,256]{1,0:T(8,128)S(1)} %get-tuple-element.19.refs_2_) | copy-start | bytes 95236
  45.5 0.5 %copy-start.9 = (f32[1,256]{1,0:T(1,128)}, f32[1,256]{1,0:T(1,128)S(1)}, u32[]{:S(2)}) copy-start(f32[1,256]{1,0:T(1,128)S(1)} %get-tuple-element.20.refs_3_) | copy-start | bytes 3076
  45.5 0.6 %copy-start.10 = (f32[1,256]{1,0:T(1,128)}, f32[1,256]{1,0:T(1,128)S(1)}, u32[]{:S(2)}) copy-start(f32[1,256]{1,0:T(1,128)S(1)} %get-tuple-element.21.refs_4_) | copy-start | bytes 3076

commit v3 on v2

--- a/solution.py
+++ b/solution.py
@@ -144,7 +144,7 @@
     st1, st1_s, st1_r, st2, st2_s, st2_r,
     f_s, f_r, fs_sem, fr_sem,
     d_s, d_r, ds_sem, dr_sem, e_r, es_sem, er_sem,
-    *ring_refs,
+    gsh, csh, *ring_refs,
 ):
     out_ring = ring_refs[:9]
     in_rings = [ring_refs[i:i + 9] for i in range(9, len(ring_refs), 9)]
@@ -267,13 +267,17 @@
     cpad[GAP + rows:] = pad
     gpad[GAP:GAP + rows] = (v * g * live[...]).astype(jnp.bfloat16).astype(jnp.float32)
 
+    span = rows + GAP + 8
+    for j in range(8):
+        gsh[j] = gpad[j:j + span]
+
     half = rows // 2
     chunks = [(a, c) for a in range(0, rows, half) for c in range(0, chans, 128)]
     for a, c in chunks:
         acc = jnp.zeros((half, 128), jnp.float32)
         for k in range(tap_count):
             first = GAP + a + k - radius
-            acc = acc + taps[k:k + 1, c:c + 128] * gpad[first:first + half, c:c + 128]
+            acc = acc + taps[k:k + 1, c:c + 128] * gsh[first % 8, first - first % 8:first - first % 8 + half, c:c + 128]
         conv[a:a + half, c:c + 128] = acc * live[a:a + half, c:c + 128]
     cv = conv[...]
     zero6 = jnp.zeros((6, chans), jnp.float32)
@@ -326,11 +330,13 @@
 
     for i, ring in enumerate(in_rings):
         c = i * 128
+        for j in range(8):
+            csh[j, :, c:c + 128] = cpad[j:j + span, c:c + 128]
         for a in range(0, rows, half):
             acc = jnp.zeros((half, 128), jnp.float32)
             for k in range(tap_count):
                 first = GAP + a + radius - k
-                acc = acc + taps[k:k + 1, c:c + 128] * cpad[first:first + half, c:c + 128]
+                acc = acc + taps[k:k + 1, c:c + 128] * csh[first % 8, first - first % 8:first - first % 8 + half, c:c + 128]
             acc = acc * live[a:a + half, c:c + 128]
             gt = gate[a:a + half, c:c + 128]
             gval = acc * gt
@@ -354,7 +360,7 @@
         for k in range(tap_count):
             first = GAP + k - radius
             d_s[k // per, k % per:k % per + 1, c:c + 128] = jnp.sum(
-                grad_c * gpad[first:first + rows, c:c + 128], axis=0, keepdims=True
+                grad_c * gsh[first % 8, first - first % 8:first - first % 8 + rows, c:c + 128], axis=0, keepdims=True
             )
 
     def d_copy(k):
@@ -419,8 +425,13 @@
 
 def hand_on(*refs):
     half = len(refs) // 2
-    for src, dst in zip(refs[:half], refs[half:]):
-        dst[...] = src[...]
+    copies = [
+        pltpu.make_async_copy(refs[i], refs[half + i], refs[-1].at[i]) for i in range(half)
+    ]
+    for copy in copies:
+        copy.start()
+    for copy in copies:
+        copy.wait()
 
 
 def fused_shards(
@@ -468,6 +479,7 @@
             dma((n_mp,)), dma((n_mp,)),
             vm((n_dp, per8, chans), f32), vm((n_dp, per8, chans), f32), *sem_pair,
             vm((n_dp, per8, chans), f32), *sem_pair,
+            vm((8, rows + GAP + 8, chans), f32), vm((8, rows + GAP + 8, chans), f32),
             *ring(chans), *(ref for _ in range(chans // 128) for ref in ring(256)),
         ],
         compiler_params=pltpu.CompilerParams(
@@ -483,8 +495,9 @@
             jax.ShapeDtypeStruct(x.shape, x.dtype)
             for x in (frame_grad, out_grad, depth_grad, gain_grad, shift_grad)
         ],
-        in_specs=[in_vmem] * 5,
-        out_specs=[in_vmem] * 5,
+        in_specs=[pl.BlockSpec(memory_space=pl.ANY)] * 5,
+        out_specs=[pl.BlockSpec(memory_space=pl.ANY)] * 5,
+        scratch_shapes=[dma((5,))],
     )(frame_grad, out_grad, depth_grad, gain_grad, shift_grad)
     return (
         frame_grad, in_flat.reshape(piece, 2, chans), out_grad, depth_grad,
@@ -498,7 +511,7 @@
     fits = (
         n_dp % 2 == 0 and n_dp <= 16 and frames.shape[1] % (128 * n_dp) == 0
         and proj_in.shape[2] % 128 == 0 and frames.shape[0] % 16 == 0
-        and taps.shape[0] // 2 <= GAP
+        and taps.shape[0] // 2 < GAP
     )
     return (fused_shards if fits else shards)(*args)
 

time: 48.8 us -> 57 us (1.17)
  Pallas kernels: 42.3 us -> 50.5 us
    pallas_call x1, Pallas kernels: 1.69 us -> 10.1 us  [fused_shards(): pl.pallas_call(hand_on, out_shape=[jax.ShapeDtypeStruct(x.shape, x.dtype)...]
where the time goes in v3:
time: 57 us; the launch traced here: 56.8 us
  Pallas kernels  50.5 us (89%)
  local copies, waits for them, and re-layouts  5.57 us (10%)
  between operations  0.77 us (1%)
    pallas_call x1, Pallas kernels, fused_shards(): pl.pallas_call(functools.partial(fused, n_dp, n_mp), out_shape=[jax.Shape...  40.3 us
    pallas_call x1, Pallas kernels, fused_shards(): pl.pallas_call(hand_on, out_shape=[jax.ShapeDtypeStruct(x.shape, x.dtype)...  10.1 us
    unnamed x27, local copies, waits for them, and re-layouts  4.71 us

profile of v3, /device:TPU:0, one launch (start us, length us, event | category | flops | bytes accessed | tf_op | source)
XLA Modules:
  0.0 56.8 jit_solution(18372949117381367579)
XLA Ops:
  0.6 0.0 copy-start
  0.6 0.0 copy-start.1
  0.7 0.0 copy-start.2
  0.7 0.0 copy-start.5
  0.7 0.0 copy-start.8
  0.7 0.0 copy-start.12
  0.7 1.6 %copy.15 = bf16[128,8,2,256]{3,1,2,0:T(8,128)(2,1)S(1)} copy(bf16[128,8,2,256]{3,2,1,0:T(2,128)(2,1)} %bitcast.9) | data formatting | bytes 2097152
  2.3 0.0 copy-start.7
  2.3 0.0 copy-start.11
  2.3 0.0 copy-done
  2.3 0.0 copy-done.1
  2.3 0.0 copy-done.2
  2.3 0.0 copy-done.5
  2.3 0.0 copy-done.8
  2.3 0.0 copy-done.12
  2.3 0.6 %copy-done.7 = f32[256]{0:T(256)S(1)} copy-done((f32[256]{0:T(256)S(1)}, f32[256]{0:T(256)}, u32[]{:S(2)}) %copy-start.7) | copy-done | bytes 1048
  3.0 0.0 copy-done.11
  3.0 40.3 %shard_map.136 = (bf16[256,256]{1,0:T(8,128)(2,1)S(1)}, f32[128,512]{1,0:T(8,128)S(1)}, f32[128,256]{1,0:T(8,128)S(1)}, f32[31,256]{1,0:T(8,128)S(1)}, f32[1,256]{1,0:T(1,128)S(1)}, /*index=5*/f32[1,256]{1,0:T(1,128)S(1)}) custom-call(bf16[256,1024]{1,0:T(8,128)(2,1)S(1)} %copy-done, bf16[1024,512]{1,0:T(8,128)(2,1)S(1)} %bitcast.6, ...), custom_call_target="tpu_custom_call" | custom-call | tf_op jit(solution)/shard_map/pallas_call | solution.py:462
  43.3 0.0 copy-start.3
  43.3 0.6 %copy-done.3 = bf16[256,256]{1,0:T(8,128)(2,1)} copy-done((bf16[256,256]{1,0:T(8,128)(2,1)}, bf16[256,256]{1,0:T(8,128)(2,1)S(1)}, u32[]{:S(2)}) %copy-start.3) | copy-done | bytes 131096
  43.9 0.0 copy-start.4
  43.9 0.6 %copy-done.4 = f32[128,256]{1,0:T(8,128)} copy-done((f32[128,256]{1,0:T(8,128)}, f32[128,256]{1,0:T(8,128)S(1)}, u32[]{:S(2)}) %copy-start.4) | copy-done | bytes 131096
  44.6 0.0 copy-start.6
  44.6 0.6 %copy-done.6 = f32[31,256]{1,0:T(8,128)} copy-done((f32[31,256]{1,0:T(8,128)}, f32[31,256]{1,0:T(8,128)S(1)}, u32[]{:S(2)}) %copy-start.6) | copy-done | bytes 31768
  45.2 0.0 copy-start.9
  45.2 0.0 copy-start.10
  45.2 0.5 copy-done.9
  45.7 0.1 copy-done.10
  45.8 10.1 %shard_map.137 = (bf16[256,256]{1,0:T(8,128)(2,1)}, f32[128,256]{1,0:T(8,128)}, f32[31,256]{1,0:T(8,128)}, f32[1,256]{1,0:T(1,128)}, f32[1,256]{1,0:T(1,128)}) custom-call(bf16[256,256]{1,0:T(8,128)(2,1)} %copy-done.3, f32[128,256]{1,0:T(8,128)} %copy-done.4, f32[31,256]{1,0:T(8,128)} %copy-done.6, f32[1,256]{1,0:T(1,128)} %copy-done.9, f32[1,256]{1,0:T(1,128)} %copy-done.10), custom_call_target="tpu_custom_call" | custom-call | tf_op jit(solution)/shard_map/pallas_call | solution.py:492
  55.9 0.9 %reshape.25 = f32[128,2,256]{2,1,0:T(2,128)} reshape(f32[128,512]{1,0:T(8,128)S(1)} %get-tuple-element.23) | data formatting | bytes 524288 | tf_op jit(solution)/shard_map/reshape | solution.py:503
Async XLA Ops:
  0.6 1.6 %copy-start = (bf16[256,1024]{1,0:T(8,128)(2,1)S(1)}, bf16[256,1024]{1,0:T(8,128)(2,1)}, u32[]{:S(2)}) copy-start(bf16[256,1024]{1,0:T(8,128)(2,1)} %frames.1) | copy-start | bytes 1572868
  0.6 1.6 %copy-start.1 = (bf16[1024,256]{1,0:T(8,128)(2,1)S(1)}, bf16[1024,256]{1,0:T(8,128)(2,1)}, u32[]{:S(2)}) copy-start(bf16[1024,256]{1,0:T(8,128)(2,1)} %proj_out.1) | copy-start | bytes 1572868
  0.7 1.7 %copy-start.2 = (bf16[256,1024]{1,0:T(8,128)(2,1)S(1)}, bf16[256,1024]{1,0:T(8,128)(2,1)}, u32[]{:S(2)}) copy-start(bf16[256,1024]{1,0:T(8,128)(2,1)} %grad_out.1) | copy-start | bytes 1572868
  0.7 1.6 %copy-start.5 = (f32[31,256]{1,0:T(8,128)S(1)}, f32[31,256]{1,0:T(8,128)}, u32[]{:S(2)}) copy-start(f32[31,256]{1,0:T(8,128)} %taps.1) | copy-start | bytes 95236
  0.7 1.6 %copy-start.8 = (f32[256]{0:T(256)S(1)}, f32[256]{0:T(256)}, u32[]{:S(2)}) copy-start(f32[256]{0:T(256)} %param.13) | copy-start | bytes 3076
  0.7 1.6 %copy-start.12 = (s32[1,2]{1,0:T(1,128)S(1)}, s32[1,2]{1,0:T(1,128)}, u32[]{:S(2)}) copy-start(s32[1,2]{1,0:T(1,128)} %lengths.1) | copy-start | bytes 28
  2.3 0.7 %copy-start.7 = (f32[256]{0:T(256)S(1)}, f32[256]{0:T(256)}, u32[]{:S(2)}) copy-start(f32[256]{0:T(256)} %param.12) | copy-start | bytes 3076
  2.3 0.7 %copy-start.11 = (s32[8]{0:T(128)S(1)}, s32[8]{0:T(128)}, u32[]{:S(2)}) copy-start(s32[8]{0:T(128)} %counts.1) | copy-start | bytes 100
  43.3 0.7 %copy-start.3 = (bf16[256,256]{1,0:T(8,128)(2,1)}, bf16[256,256]{1,0:T(8,128)(2,1)S(1)}, u32[]{:S(2)}) copy-start(bf16[256,256]{1,0:T(8,128)(2,1)S(1)} %get-tuple-element.17.refs_0_) | copy-start | bytes 393220
  43.9 0.6 %copy-start.4 = (f32[128,256]{1,0:T(8,128)}, f32[128,256]{1,0:T(8,128)S(1)}, u32[]{:S(2)}) copy-start(f32[128,256]{1,0:T(8,128)S(1)} %get-tuple-element.18.refs_1_) | copy-start | bytes 393220
  44.6 0.6 %copy-start.6 = (f32[31,256]{1,0:T(8,128)}, f32[31,256]{1,0:T(8,128)S(1)}, u32[]{:S(2)}) copy-start(f32[31,256]{1,0:T(8,128)S(1)} %get-tuple-element.19.refs_2_) | copy-start | bytes 95236
  45.2 0.5 copy-start.9
  45.2 0.6 %copy-start.10 = (f32[1,256]{1,0:T(1,128)}, f32[1,256]{1,0:T(1,128)S(1)}, u32[]{:S(2)}) copy-start(f32[1,256]{1,0:T(1,128)S(1)} %get-tuple-element.21.refs_4_) | copy-start | bytes 3076

commit v4 on v3

--- a/solution.py
+++ b/solution.py
@@ -421,17 +421,6 @@
         f_copy(k).wait_send()
     for k in range(1, n_dp):
         d_copy(k).wait_send()
-
-
-def hand_on(*refs):
-    half = len(refs) // 2
-    copies = [
-        pltpu.make_async_copy(refs[i], refs[half + i], refs[-1].at[i]) for i in range(half)
-    ]
-    for copy in copies:
-        copy.start()
-    for copy in copies:
-        copy.wait()
 
 
 def fused_shards(
@@ -489,16 +478,6 @@
         frames, proj_in.reshape(width, 2 * chans), depthwise, bn_gain[None], bn_shift[None],
         proj_out, grad_out, counts, lengths,
     )
-    frame_grad, out_grad, depth_grad, gain_grad, shift_grad = pl.pallas_call(
-        hand_on,
-        out_shape=[
-            jax.ShapeDtypeStruct(x.shape, x.dtype)
-            for x in (frame_grad, out_grad, depth_grad, gain_grad, shift_grad)
-        ],
-        in_specs=[pl.BlockSpec(memory_space=pl.ANY)] * 5,
-        out_specs=[pl.BlockSpec(memory_space=pl.ANY)] * 5,
-        scratch_shapes=[dma((5,))],
-    )(frame_grad, out_grad, depth_grad, gain_grad, shift_grad)
     return (
         frame_grad, in_flat.reshape(piece, 2, chans), out_grad, depth_grad,
         gain_grad.reshape(chans), shift_grad.reshape(chans),

time: 57 us -> 47.4 us (0.83)
  Pallas kernels: 50.5 us -> 40.3 us
    pallas_call x1 -> x0, Pallas kernels: 10.1 us -> none  [fused_shards(): pl.pallas_call(hand_on, out_shape=[jax.ShapeDtypeStruct(x.shape, x.dtype)...]
    unnamed x27 -> x22, local copies, waits for them, and re-layouts: 4.71 us -> 5.26 us
where the time goes in v4:
time: 47.4 us; the launch traced here: 47.2 us
  Pallas kernels  40.3 us (85%)
  local copies, waits for them, and re-layouts  6.13 us (13%)
  between operations  0.75 us (2%)
    pallas_call x1, Pallas kernels, fused_shards(): pl.pallas_call(functools.partial(fused, n_dp, n_mp), out_shape=[jax.Shape...  40.3 us
    unnamed x22, local copies, waits for them, and re-layouts  5.26 us

profile of v4, /device:TPU:0, one launch (start us, length us, event | category | flops | bytes accessed | tf_op | source)
XLA Modules:
  0.0 47.2 jit_solution(16975606737653310911)
XLA Ops:
  0.6 0.0 copy-start
  0.6 0.0 copy-start.1
  0.7 0.0 copy-start.2
  0.7 0.0 copy-start.3
  0.7 0.0 copy-start.5
  0.7 0.0 copy-start.7
  0.7 1.6 %copy.15 = bf16[128,8,2,256]{3,1,2,0:T(8,128)(2,1)S(1)} copy(bf16[128,8,2,256]{3,2,1,0:T(2,128)(2,1)} %bitcast.11) | data formatting | bytes 2097152
  2.3 0.0 copy-start.4
  2.3 0.0 copy-start.6
  2.3 0.0 copy-done
  2.3 0.0 copy-done.1
  2.3 0.0 copy-done.2
  2.3 0.0 copy-done.3
  2.3 0.0 copy-done.5
  2.3 0.0 copy-done.7
  2.3 0.6 %copy-done.4 = f32[256]{0:T(256)S(1)} copy-done((f32[256]{0:T(256)S(1)}, f32[256]{0:T(256)}, u32[]{:S(2)}) %copy-start.4) | copy-done | bytes 1048
  3.0 0.0 copy-done.6
  3.0 40.3 %shard_map.136 = (bf16[256,256]{1,0:T(8,128)(2,1)S(1)}, f32[128,512]{1,0:T(8,128)S(1)}, f32[128,256]{1,0:T(8,128)S(1)}, f32[31,256]{1,0:T(8,128)S(1)}, f32[1,256]{1,0:T(1,128)S(1)}, /*index=5*/f32[1,256]{1,0:T(1,128)S(1)}) custom-call(bf16[256,1024]{1,0:T(8,128)(2,1)S(1)} %copy-done, bf16[1024,512]{1,0:T(8,128)(2,1)S(1)} %bitcast.6, ...), custom_call_target="tpu_custom_call" | custom-call | tf_op jit(solution)/shard_map/pallas_call | solution.py:451
  43.3 0.9 %reshape.25 = f32[128,2,256]{2,1,0:T(2,128)} reshape(f32[128,512]{1,0:T(8,128)S(1)} %get-tuple-element.13) | data formatting | bytes 524288 | tf_op jit(solution)/shard_map/reshape | solution.py:482
  44.1 0.7 %copy.21 = bf16[256,256]{1,0:T(8,128)(2,1)} copy(bf16[256,256]{1,0:T(8,128)(2,1)S(1)} %get-tuple-element.24) | data formatting | bytes 262144
  44.8 0.7 %copy.22 = f32[128,256]{1,0:T(8,128)} copy(f32[128,256]{1,0:T(8,128)S(1)} %get-tuple-element.26) | data formatting | bytes 262144
  45.5 0.6 %copy.23 = f32[31,256]{1,0:T(8,128)} copy(f32[31,256]{1,0:T(8,128)S(1)} %get-tuple-element.27) | data formatting | bytes 63488
  46.1 0.6 %copy.24 = f32[256]{0:T(256)} copy(f32[256]{0:T(256)S(1)} %bitcast.10) | data formatting | bytes 2048
  46.6 0.6 %copy.25 = f32[256]{0:T(256)} copy(f32[256]{0:T(256)S(1)} %bitcast.9) | data formatting | bytes 2048
Async XLA Ops:
  0.6 1.6 %copy-start = (bf16[256,1024]{1,0:T(8,128)(2,1)S(1)}, bf16[256,1024]{1,0:T(8,128)(2,1)}, u32[]{:S(2)}) copy-start(bf16[256,1024]{1,0:T(8,128)(2,1)} %frames.1) | copy-start | bytes 1572868
  0.6 1.6 %copy-start.1 = (bf16[1024,256]{1,0:T(8,128)(2,1)S(1)}, bf16[1024,256]{1,0:T(8,128)(2,1)}, u32[]{:S(2)}) copy-start(bf16[1024,256]{1,0:T(8,128)(2,1)} %proj_out.1) | copy-start | bytes 1572868
  0.7 1.7 %copy-start.2 = (bf16[256,1024]{1,0:T(8,128)(2,1)S(1)}, bf16[256,1024]{1,0:T(8,128)(2,1)}, u32[]{:S(2)}) copy-start(bf16[256,1024]{1,0:T(8,128)(2,1)} %grad_out.1) | copy-start | bytes 1572868
  0.7 1.6 %copy-start.3 = (f32[31,256]{1,0:T(8,128)S(1)}, f32[31,256]{1,0:T(8,128)}, u32[]{:S(2)}) copy-start(f32[31,256]{1,0:T(8,128)} %taps.1) | copy-start | bytes 95236
  0.7 1.6 %copy-start.5 = (f32[256]{0:T(256)S(1)}, f32[256]{0:T(256)}, u32[]{:S(2)}) copy-start(f32[256]{0:T(256)} %param.13) | copy-start | bytes 3076
  0.7 1.6 %copy-start.7 = (s32[1,2]{1,0:T(1,128)S(1)}, s32[1,2]{1,0:T(1,128)}, u32[]{:S(2)}) copy-start(s32[1,2]{1,0:T(1,128)} %lengths.1) | copy-start | bytes 28
  2.3 0.7 %copy-start.4 = (f32[256]{0:T(256)S(1)}, f32[256]{0:T(256)}, u32[]{:S(2)}) copy-start(f32[256]{0:T(256)} %param.12) | copy-start | bytes 3076
  2.3 0.7 %copy-start.6 = (s32[8]{0:T(128)S(1)}, s32[8]{0:T(128)}, u32[]{:S(2)}) copy-start(s32[8]{0:T(128)} %counts.1) | copy-start | bytes 100
